TPU v7x, 256 devices: a whole 4x4x8 slice. The times are simulated.
256 devices in a mesh: lon: 16 (over y_hi, z), lat: 16 (over x, y_lo, core).
Axes of the slice: x: 4, y: 4 (y_hi: 2, y_lo: 2; y = y_hi * 2 + y_lo), z: 8, core: 2. Of those that a mesh axis runs over, the one named last changes fastest.
Arguments:
- u_velocity: float32 [12, 1536, 2048], P(None, 'lat', 'lon'), may hold values from -6 to 6
- v_velocity: float32 [12, 1536, 2048], P(None, 'lat', 'lon'), may hold values from -6 to 6
- density: float32 [12, 1536, 2048], P(None, 'lat', 'lon'), may hold values from -6 to 6
- surface: float32 [1536, 2048], P('lat', 'lon'), may hold values from -4 to 4
- land_mask: int32 [12, 1536, 2048], P(None, 'lat', 'lon'), may hold values from 0 to 1, as said below
- bottom: int32 [1536, 2048], P('lat', 'lon'), may hold values from 0 to 12
Outputs:
- u_final: float32 [12, 1536, 2048], P(None, 'lat', 'lon')
- v_final: float32 [12, 1536, 2048], P(None, 'lat', 'lon')
- surface_final: float32 [1536, 2048], P('lat', 'lon')
Inputs may be any that keep to these rules, and one draw needn't show every extreme that they name: land_mask is 1 only at levels above the column's bottom; in an ocean column every level from its first ocean level (0, 1 or 2) down to bottom - 1 is 1.
All inputs are finite; a program needn't handle non-finite values.
Results may differ from a plain program's by a relative error of at most 0.0003.
Values sent between devices are 32-bit elements; how exact they have to be, the bound alone decides.
No kernel may reach another device: no remote copies, remote signals or barrier semaphores. Data moves between devices by JAX's collectives and lax.ppermute only.
A program may use at most 64 MiB of HBM per device.

v0:
```python
import math

import jax
import jax.numpy as jnp
from jax import lax
from jax.sharding import PartitionSpec as P

SUBSTEPS = 8
STEPS = 2


gravity = 1.0
buoyancy = 1.0
viscosity = 0.05
friction = 0.1
coriolis = 0.25
substep_time = 0.4


def partner_2(block, axis, apart):
    count = lax.axis_size(axis)
    route = []
    for low in range(count):
        high = low | 1 << apart
        if high != low and high < count:
            route += [(low, high), (high, low)]
    return lax.ppermute(block, axis, route)


def extended(cells, sides, width):
    for axis, dim in sides:
        count = lax.axis_size(axis)
        head = lax.slice_in_dim(cells, 0, width, axis=dim)
        tail = lax.slice_in_dim(cells, cells.shape[dim] - width, cells.shape[dim], axis=dim)
        cells = jnp.concatenate(
            [
                lax.ppermute(tail, axis, [(i, (i + 1) % count) for i in range(count)]),
                cells,
                lax.ppermute(head, axis, [((i + 1) % count, i) for i in range(count)]),
            ],
            axis=dim,
        )
    return cells


def east_part(padded):
    return padded[..., 1:-1, 2:]


def west_part(padded):
    return padded[..., 1:-1, :-2]


def north_part(padded):
    return padded[..., 2:, 1:-1]


def south_part(padded):
    return padded[..., :-2, 1:-1]


def corner_south_east(padded):
    return padded[..., :-2, 2:]


def corner_north_west(padded):
    return padded[..., 2:, :-2]


def mirrored(partner, kinds):
    pieces = []
    for place, kind in enumerate(kinds):
        flipped = jnp.flip(partner[place], -1)
        if kind == "t":
            pieces.append(flipped)
        elif kind == "v":
            pieces.append(-flipped)
        else:
            shifted = jnp.concatenate([flipped[..., 1:], jnp.zeros_like(flipped[..., :1])], axis=-1)
            pieces.append(-shifted)
    return jnp.stack(pieces)


def fetch_mirror(seam_rows, deep):
    partner = seam_rows
    for bit_number in range(lax.axis_size("lon").bit_length() - 1):
        if deep:
            partner = partner_2(partner, "lon", bit_number)
        else:
            partner = partner_2(partner, "lon", bit_number)
    return partner


def fix_edges(padded, ghost):
    summit = lax.axis_index("lat") == lax.axis_size("lat") - 1
    upper = jnp.where(summit, ghost, padded[..., -1, :])
    base = lax.axis_index("lat") == 0
    lower = jnp.where(base, jnp.zeros_like(padded[..., 0, :]), padded[..., 0, :])
    return jnp.concatenate(
        [lower[..., None, :], padded[..., 1:-1, :], upper[..., None, :]], axis=-2
    )


def fold_rows(padded, kinds, deep):
    partner = fetch_mirror(padded[..., -3, :], deep)
    return fix_edges(padded, mirrored(partner, kinds))


def extend_levels(stack, kinds):
    padded = extended(stack, (("lon", 3), ("lat", 2)), 1)
    return fold_rows(padded, kinds, True)


def surface_halo(stack):
    return extended(stack, (("lon", 2), ("lat", 1)), 1)


def extend_surface(stack, kinds):
    return fold_rows(surface_halo(stack), kinds, False)


def shards(u_velocity, v_velocity, density, surface, land_mask, bottom):
    levels, rows_local, cols_local = u_velocity.shape
    layer = 1.0 / levels
    lat_cells = lax.axis_size("lat") * rows_local
    row_ids = (lax.axis_index("lat") * rows_local + jnp.arange(rows_local)).astype(jnp.float32)
    spin_centre = coriolis * jnp.sin(math.pi * ((row_ids + 0.5) / lat_cells - 0.5))[:, None]
    spin_face = coriolis * jnp.sin(math.pi * ((row_ids + 1.0) / lat_cells - 0.5))[:, None]
    floor_here = bottom.astype(jnp.float32)
    floor_wide = extend_surface(floor_here[None], ("t",))[0]
    floor_east = east_part(floor_wide)
    floor_north = north_part(floor_wide)
    level_ids = jnp.arange(levels, dtype=jnp.float32)[:, None, None]
    ocean = land_mask.astype(jnp.float32)
    u_mask = ocean * (level_ids < floor_east).astype(jnp.float32)
    v_mask = ocean * (level_ids < floor_north).astype(jnp.float32)
    sea_cells = (floor_here > 0.0).astype(jnp.float32)
    u_wet = jnp.max(u_mask, axis=0)
    v_wet = jnp.max(v_mask, axis=0)
    u_depth = layer * jnp.sum(u_mask, axis=0)
    v_depth = layer * jnp.sum(v_mask, axis=0)
    step_time = SUBSTEPS * substep_time
    drag = 1.0 / (1.0 + step_time * friction)
    u_drag = jnp.where(level_ids == jnp.minimum(floor_here, floor_east) - 1.0, drag, 1.0).astype(
        jnp.float32
    )
    v_drag = jnp.where(level_ids == jnp.minimum(floor_here, floor_north) - 1.0, drag, 1.0).astype(
        jnp.float32
    )
    weighted = ocean * density
    pressure = buoyancy * layer * (jnp.cumsum(weighted, axis=0) - 0.5 * weighted)
    u_now = u_velocity * u_mask
    v_now = v_velocity * v_mask
    height = surface * sea_cells
    grad_u = jnp.zeros_like(pressure)
    grad_v = jnp.zeros_like(pressure)
    for step in range(STEPS):
        if step == 0:
            padded = extend_levels(jnp.stack([u_now, v_now, pressure]), ("u", "v", "t"))
            grad_u = east_part(padded[2]) - pressure
            grad_v = north_part(padded[2]) - pressure
        else:
            padded = extend_levels(jnp.stack([u_now, v_now]), ("u", "v"))
        wide_u = padded[0]
        wide_v = padded[1]
        lap_u = (
            east_part(wide_u)
            + west_part(wide_u)
            + north_part(wide_u)
            + south_part(wide_u)
            - 4.0 * u_now
        )
        lap_v = (
            east_part(wide_v)
            + west_part(wide_v)
            + north_part(wide_v)
            + south_part(wide_v)
            - 4.0 * v_now
        )
        v_at_u = 0.25 * (v_now + east_part(wide_v) + south_part(wide_v) + corner_south_east(wide_v))
        u_at_v = 0.25 * (u_now + west_part(wide_u) + north_part(wide_u) + corner_north_west(wide_u))
        tend_u = u_mask * (-grad_u + spin_centre * v_at_u + viscosity * lap_u)
        tend_v = v_mask * (-grad_v - spin_face * u_at_v + viscosity * lap_v)
        force_u = layer * jnp.sum(tend_u, axis=0)
        force_v = layer * jnp.sum(tend_v, axis=0)
        flow_u = layer * jnp.sum(u_now, axis=0)
        flow_v = layer * jnp.sum(v_now, axis=0)

        def advance_flows(
            east_flow, north_flow, flow_east, flow_north, level, level_east, level_north
        ):
            flow_at_u = 0.25 * (
                north_flow
                + east_part(flow_north)
                + south_part(flow_north)
                + corner_south_east(flow_north)
            )
            flow_at_v = 0.25 * (
                east_flow
                + west_part(flow_east)
                + north_part(flow_east)
                + corner_north_west(flow_east)
            )
            next_u = u_wet * (
                east_flow
                + substep_time
                * (-gravity * u_depth * (level_east - level) + spin_centre * flow_at_u + force_u)
            )
            next_v = v_wet * (
                north_flow
                + substep_time
                * (-gravity * v_depth * (level_north - level) - spin_face * flow_at_v + force_v)
            )
            return (next_u, next_v)

        def substep_twice(turn, carry):
            level, east_flow, north_flow, total_u, total_v = carry
            wide_flow = extend_surface(jnp.stack([east_flow, north_flow]), ("u", "v"))
            flow_east = wide_flow[0]
            flow_north = wide_flow[1]
            level = sea_cells * (
                level
                - substep_time
                * (east_flow - west_part(flow_east) + north_flow - south_part(flow_north))
            )
            wide_level = extend_surface(level[None], ("t",))[0]
            next_u, next_v = advance_flows(
                east_flow,
                north_flow,
                flow_east,
                flow_north,
                level,
                east_part(wide_level),
                north_part(wide_level),
            )
            return (level, next_u, next_v, total_u + next_u, total_v + next_v)

        start = (height, flow_u, flow_v, jnp.zeros_like(flow_u), jnp.zeros_like(flow_v))
        height, flow_u, flow_v, total_u, total_v = lax.fori_loop(0, SUBSTEPS, substep_twice, start)
        mean_u = total_u / SUBSTEPS
        mean_v = total_v / SUBSTEPS
        new_u = u_drag * (u_now + step_time * tend_u)
        new_v = v_drag * (v_now + step_time * tend_v)
        u_now = u_mask * (
            new_u + (mean_u - layer * jnp.sum(new_u, axis=0)) / jnp.maximum(u_depth, layer)
        )
        v_now = v_mask * (
            new_v + (mean_v - layer * jnp.sum(new_v, axis=0)) / jnp.maximum(v_depth, layer)
        )
    return (u_now, v_now, height)


def solution(mesh):
    return jax.shard_map(
        shards,
        mesh=mesh,
        in_specs=(
            P(None, "lat", "lon"),
            P(None, "lat", "lon"),
            P(None, "lat", "lon"),
            P("lat", "lon"),
            P(None, "lat", "lon"),
            P("lat", "lon"),
        ),
        out_specs=(P(None, "lat", "lon"), P(None, "lat", "lon"), P("lat", "lon")),
        check_vma=False,
    )
```

profile of v0, /device:TPU:7, one launch (start us, length us, event | category | flops | bytes accessed | tf_op | source)
XLA Modules:
  0.0 1108.4 jit_solution(7200126055340907075)
XLA Ops:
  101.7 472.5 %while.42 = (s32[]{:T(128)}, f32[96,128]{1,0:T(8,128)S(1)}, f32[96,128]{1,0:T(8,128)S(1)}, f32[96,128]{1,0:T(8,128)S(1)}, f32[96,128]{1,0:T(8,128)S(1)}, /*index...) while((s32[]{:T(128)}, f32[96,128]{1,0:T(8,128)S(1)}, ...), condition=%wide.region_10.11_spmd.clone.clone.clone, body=%wide.region_9.10_spmd.clone.clone.clone.sunk | while | flops 602246 | bytes 2556030 | solution.py:239
  116.6 8.8 collective-permute-start.7
  146.2 8.4 collective-permute-start.15
  205.4 8.4 collective-permute-start.15
  264.7 8.4 collective-permute-start.15
  501.7 8.4 collective-permute-start.15
  603.1 8.5 collective-permute-start.50
  628.3 474.7 %while.43 = (s32[]{:T(128)}, f32[96,128]{1,0:T(8,128)S(1)}, f32[96,128]{1,0:T(8,128)S(1)}, f32[96,128]{1,0:T(8,128)S(1)}, f32[96,128]{1,0:T(8,128)S(1)}, /*index...) while((s32[]{:T(128)}, f32[96,128]{1,0:T(8,128)S(1)}, ...), condition=%wide.region_18.19_spmd.clone.clone.clone, body=%wide.region_17.18_spmd.clone.clone.clone.sunk | while | flops 602246 | bytes 2556030 | solution.py:239
  645.5 8.7 collective-permute-start.23
  675.1 8.5 collective-permute-start.31
  705.0 8.5 collective-permute-start.23
  734.4 8.5 collective-permute-start.31
  764.3 8.5 collective-permute-start.23
  793.6 8.5 collective-permute-start.31
  823.5 8.5 collective-permute-start.23
  852.9 8.5 collective-permute-start.31
  882.8 8.5 collective-permute-start.23
  912.1 8.5 collective-permute-start.31
  942.0 8.5 collective-permute-start.23
  971.4 8.5 collective-permute-start.31
  1001.3 8.5 collective-permute-start.23
  1030.6 8.5 collective-permute-start.31
  1060.5 8.5 collective-permute-start.23
  1089.9 8.5 collective-permute-start.31
  (1062 shorter events, 917.5 us)
Async XLA Ops:
  60.5 17.2 %collective-permute-start.42 = (f32[3,12,1,130]{3,1,2,0:T(8,128)}, f32[3,12,1,130]{3,1,2,0:T(8,128)}, u32[]{:S(2)}, u32[]{:S(2)}) collective-permute-start(f32[3,12,1,130]{3,1,2,0:T(8,128)} %get-tuple-element.537), channel_id=1, source_target_pairs={{0,1},{1,2},{2,3},{3,4},{4,5},{5,6},{6,7},{7,8},{8,9},{9,10},{10,1... | collective-permute-start | bytes 56168 | tf_op jit(solution)/shard_map/ppermute | solution.py:37
  69.1 18.8 %collective-permute-start.47 = (f32[3,12,1,130]{3,1,2,0:T(8,128)}, f32[3,12,1,130]{3,1,2,0:T(8,128)}, u32[]{:S(2)}, u32[]{:S(2)}) collective-permute-start(f32[3,12,1,130]{3,1,2,0:T(8,128)} %get-tuple-element.539), channel_id=1, source_target_pairs={{1,0},{2,1},{3,2},{4,3},{5,4},{6,5},{7,6},{8,7},{9,8},{10,9},{11,1... | collective-permute-start | bytes 56168 | tf_op jit(solution)/shard_map/ppermute | solution.py:39
  116.6 10.7 collective-permute-start.7
  324.0 10.5 collective-permute-start.15
  383.2 10.5 collective-permute-start.15
  442.5 10.5 collective-permute-start.15
  501.7 10.5 collective-permute-start.15
  561.0 10.5 collective-permute-start.15
  603.1 10.6 collective-permute-start.50
  645.5 10.7 collective-permute-start.23
  705.0 10.5 collective-permute-start.23
  734.4 10.5 collective-permute-start.31
  764.3 10.5 collective-permute-start.23
  793.6 10.5 collective-permute-start.31
  823.5 10.5 collective-permute-start.23
  852.9 10.5 collective-permute-start.31
  882.8 10.5 collective-permute-start.23
  912.1 10.5 collective-permute-start.31
  942.0 10.5 collective-permute-start.23
  971.4 10.5 collective-permute-start.31
  1001.3 10.5 collective-permute-start.23
  1030.6 10.5 collective-permute-start.31
  1060.5 10.5 collective-permute-start.23
  1089.9 10.5 collective-permute-start.31
  (280 other events, 4816.2 us)
where the time goes:
time: 1130 us; the launch traced here: 1110 us
  waiting for transfers between devices  508 us (45%)
  starting transfers between devices  497 us (44%)
  other arithmetic  63.7 us (6%)
  local copies, waits for them, and re-layouts  35.6 us (3%)
    ppermute x70, starting transfers between devices, extended(): lax.ppermute(tail, axis, [(i, (i + 1) % count) for i in range(count)])  293 us
    ppermute x140, waiting for transfers between devices, partner_2(): return lax.ppermute(block, axis, route)  275 us
    ppermute x70, waiting for transfers between devices, extended(): lax.ppermute(tail, axis, [(i, (i + 1) % count) for i in range(count)])  186 us
    ppermute x70, starting transfers between devices, extended(): lax.ppermute(head, axis, [((i + 1) % count, i) for i in range(count)])  133 us
    ppermute x140, starting transfers between devices, partner_2(): return lax.ppermute(block, axis, route)  71.6 us
    ppermute x70, waiting for transfers between devices, extended(): lax.ppermute(head, axis, [((i + 1) % count, i) for i in range(count)])  46.8 us
  transfers between devices with their start and end apart: 280, of which 175 were waited for; matrix products, arithmetic and copies ran while one was open for 2% of the time, Pallas kernels for 0%

commit v1 on v0

v1 whole, which is shorter than its diff:
```python
import math

import jax
import jax.numpy as jnp
from jax import lax
from jax.experimental import pallas as pl
from jax.experimental.pallas import tpu as pltpu
from jax.sharding import PartitionSpec as P

SUBSTEPS = 8
STEPS = 2
LEVELS = 12
ROWS = 96
LANES = 128
HALO = 16
FOLD = 18

PLANES = 3 * LEVELS + 3
BOTTOM, FIRST, SURFACE = 36, 37, 38
PACKS = -(-PLANES // 8)
SENT = PLANES + 2 * PACKS

PAD = 8
EXT = 136
TALL = PAD + EXT + PAD
OWN = HALO
GHOST_A, PATCH, GHOST_B = OWN + ROWS, OWN + ROWS + 1, OWN + ROWS + 1 + FOLD
CHUNKS = ((0, 32), (32, 32), (64, 32), (96, 40))

viscosity = 0.05
friction = 0.1
coriolis = 0.25
substep_time = 0.4
layer = 1.0 / LEVELS
step_time = SUBSTEPS * substep_time
drag = 1.0 / (1.0 + step_time * friction)

VMEM_LIMIT = 56 * 1024 * 1024


def lanes_of(shape):
    return lax.broadcasted_iota(jnp.int32, shape, len(shape) - 1)


def prepare(u_ref, v_ref, d_ref, s_ref, m_ref, b_ref, own_ref, a_ref, c_ref):
    lane = lanes_of((ROWS, LANES))
    row = lax.broadcasted_iota(jnp.int32, (ROWS, LANES), 0)
    bottom = b_ref[...].astype(jnp.float32)
    ocean = [m_ref[k].astype(jnp.float32) for k in range(LEVELS)]
    first = bottom - sum(ocean)
    east = jnp.where(lane == LANES - 1, 12.0, pltpu.roll(bottom, LANES - 1, 1))
    north = jnp.where(row == ROWS - 1, 12.0, pltpu.roll(bottom, ROWS - 1, 0))
    running = jnp.zeros_like(bottom)
    for k in range(LEVELS):
        weighted = ocean[k] * d_ref[k]
        running = running + weighted
        own_ref[k] = jnp.where(east > k, ocean[k] * u_ref[k], 0.0)
        own_ref[LEVELS + k] = jnp.where(north > k, ocean[k] * v_ref[k], 0.0)
        own_ref[2 * LEVELS + k] = layer * (running - 0.5 * weighted)
    own_ref[BOTTOM] = bottom
    own_ref[FIRST] = first
    own_ref[SURFACE] = jnp.where(bottom > 0.0, s_ref[...], 0.0)
    even = lax.rem(lax.axis_index("lon"), 2) == 0
    for pack in range(PACKS):
        to_east = jnp.zeros((ROWS, LANES), jnp.float32)
        to_west = jnp.zeros((ROWS, LANES), jnp.float32)
        for slot in range(min(8, PLANES - 8 * pack)):
            plane = own_ref[8 * pack + slot]
            here = (lane >= HALO * slot) & (lane < HALO * slot + HALO)
            to_east = jnp.where(here, pltpu.roll(plane, (HALO * slot + HALO) % LANES, 1), to_east)
            moved = pltpu.roll(plane, HALO * slot, 1) if slot else plane
            to_west = jnp.where(here, moved, to_west)
        a_ref[pack] = jnp.where(even, to_east, to_west)
        c_ref[pack] = jnp.where(even, to_west, to_east)


def outer_rows(low_own, low_a, low_b, top_own, top_a, top_b, a_ref, c_ref):
    even = lax.rem(lax.axis_index("lat"), 2) == 0
    for p in range(SENT):
        if p < PLANES:
            low, top = low_own[p], top_own[p]
        elif p < PLANES + PACKS:
            low, top = low_a[p - PLANES], top_a[p - PLANES]
        else:
            low, top = low_b[p - PLANES - PACKS], top_b[p - PLANES - PACKS]
        a_ref[pl.ds(p * HALO, HALO), :] = jnp.where(even, top[24 - HALO :], low[:HALO])
        c_ref[pl.ds(p * FOLD, FOLD), :] = jnp.where(even, low[:FOLD], top[24 - FOLD :])


def eastward(t0, t1):
    lane = lanes_of(t0.shape)
    r0, r1 = pltpu.roll(t0, LANES - 1, t0.ndim - 1), pltpu.roll(t1, LANES - 1, t0.ndim - 1)
    edge = lane == LANES - 1
    return jnp.where(edge, r1, r0), jnp.where(edge, r0, r1)


def westward(t0, t1):
    lane = lanes_of(t0.shape)
    r0, r1 = pltpu.roll(t0, 1, t0.ndim - 1), pltpu.roll(t1, 1, t0.ndim - 1)
    edge = lane == 0
    return jnp.where(edge, r1, r0), jnp.where(edge, r0, r1)


def fold_ghosts(ref, top, sign=1.0):
    for t in range(2):
        for ghost, source in ((GHOST_A, PATCH + FOLD - 2), (GHOST_B, OWN + ROWS - 2)):
            kept = ref[t, pl.ds(PAD + ghost, 1), :]
            taken = ref[t, pl.ds(PAD + source, 1), :]
            ref[t, pl.ds(PAD + ghost, 1), :] = jnp.where(top, sign * taken, kept)


def ocean_steps(
    own_ref, ea_ref, eb_ref, na_ref, nb_ref, ft_ref, fv_ref,
    u_out, v_out, h_out,
    u_all, v_all, p_all, u_new, v_new,
    flat, flow_u, flow_v, height,
):
    lat = lax.axis_index("lat")
    even_lat = lax.rem(lat, 2) == 0
    even_lon = lax.rem(lax.axis_index("lon"), 2) == 0
    top = lat == lax.axis_size("lat") - 1
    a_side = jnp.where(even_lon, 0, LANES - HALO)
    b_side = jnp.where(even_lon, LANES - HALO, 0)
    (BED, FROM, UP_U, LO_U, UP_V, C_U, F_U, G_U, C_V, F_V, G_V, SUM_U, SUM_V, NEW_U, NEW_V, SEA) = range(16)

    def place(p):
        if p < LEVELS:
            return u_all.at[p]
        if p < 2 * LEVELS:
            return v_all.at[p - LEVELS]
        if p < 3 * LEVELS:
            return p_all.at[p - 2 * LEVELS]
        return {BOTTOM: flat.at[BED], FIRST: flat.at[FROM], SURFACE: height}[p]

    def side(a, b, p, shape):
        lane = lanes_of(shape)
        slot = HALO * (p % 8)
        from_a = pltpu.roll(a, lax.rem(a_side - slot + LANES, LANES), 1)
        from_b = pltpu.roll(b, lax.rem(b_side - slot + LANES, LANES), 1)
        in_a = (lane >= a_side) & (lane < a_side + HALO)
        in_b = (lane >= b_side) & (lane < b_side + HALO)
        outside = 12.0 if p in (BOTTOM, FIRST) else 0.0
        return jnp.where(in_a, from_a, jnp.where(in_b, from_b, outside))

    def north_rows(p):
        return jnp.where(even_lat, na_ref[pl.ds(p * HALO, HALO), :], nb_ref[pl.ds(p * FOLD, HALO), :])

    def south_rows(p):
        return jnp.where(even_lat, nb_ref[pl.ds(p * FOLD + FOLD - HALO, HALO), :], na_ref[pl.ds(p * HALO, HALO), :])

    for p in range(PLANES):
        ref = place(p)
        beyond = 12.0 if p in (BOTTOM, FIRST) else 0.0
        pa, pb = PLANES + p // 8, PLANES + PACKS + p // 8
        ref[0, pl.ds(PAD, HALO), :] = south_rows(p)
        ref[0, pl.ds(PAD + OWN, ROWS), :] = own_ref[p]
        ref[0, pl.ds(PAD + OWN + ROWS, HALO), :] = north_rows(p)
        ref[1, pl.ds(PAD, HALO), :] = side(south_rows(pa), south_rows(pb), p, (HALO, LANES))
        ref[1, pl.ds(PAD + OWN, ROWS), :] = side(ea_ref[p // 8], eb_ref[p // 8], p, (ROWS, LANES))
        ref[1, pl.ds(PAD + OWN + ROWS, HALO), :] = side(north_rows(pa), north_rows(pb), p, (HALO, LANES))
        for t in range(2):
            ref[t, pl.ds(0, PAD), :] = jnp.full((PAD, LANES), beyond, jnp.float32)
            ref[t, pl.ds(PAD + OWN + ROWS + HALO, 16), :] = jnp.full((16, LANES), beyond, jnp.float32)

    @pl.when(top)
    def _():
        flip_row = lax.broadcasted_iota(jnp.int32, (LANES, LANES), 0)
        flip_lane = lax.broadcasted_iota(jnp.int32, (LANES, LANES), 1)
        flip = (flip_row + flip_lane == LANES - 1).astype(jnp.float32)

        def flipped(x):
            return jnp.dot(x, flip, precision=lax.Precision.HIGHEST, preferred_element_type=jnp.float32)

        for p in range(PLANES):
            ref = place(p)
            pa, pb = PLANES + p // 8, PLANES + PACKS + p // 8
            lane = lanes_of((FOLD, LANES))
            slot = HALO * (p % 8)
            a, b = nb_ref[pl.ds(pa * FOLD, FOLD), :], nb_ref[pl.ds(pb * FOLD, FOLD), :]
            from_a = pltpu.roll(a, lax.rem(b_side - slot + LANES, LANES), 1)
            from_b = pltpu.roll(b, lax.rem(a_side - slot + LANES, LANES), 1)
            in_a = (lane >= b_side) & (lane < b_side + HALO)
            in_b = (lane >= a_side) & (lane < a_side + HALO)
            outside = 12.0 if p in (BOTTOM, FIRST) else 0.0
            beside = jnp.where(in_a, from_a, jnp.where(in_b, from_b, outside))
            t0, t1 = flipped(nb_ref[pl.ds(p * FOLD, FOLD), :]), flipped(beside)
            if p < LEVELS:
                t0, t1 = eastward(t0, t1)
                t0, t1 = -t0, -t1
            ref[0, pl.ds(PAD + PATCH, FOLD), :] = t0
            ref[1, pl.ds(PAD + PATCH, FOLD), :] = t1

    fold_ghosts(flat.at[BED], top)

    for at, n in CHUNKS:
        rows = pl.ds(PAD + at, n)
        up = pl.ds(PAD + at + 1, n)
        bed = [flat[BED, t, rows, :] for t in range(2)]
        start = [flat[FROM, t, rows, :] for t in range(2)]
        bed_east = eastward(*bed)
        start_east = eastward(*start)
        ext_row = lax.broadcasted_iota(jnp.int32, (n, LANES), 0) + at
        mirror = (ext_row >= jnp.where(top, PATCH, EXT)) & (ext_row < PATCH + FOLD)
        for t in range(2):
            up_u = jnp.minimum(bed[t], bed_east[t])
            lo_u = jnp.where(mirror, start_east[t], start[t])
            up_v = jnp.minimum(bed[t], flat[BED, t, up, :])
            count_u = jnp.maximum(up_u - lo_u, 0.0)
            count_v = jnp.maximum(up_v - start[t], 0.0)
            flat[UP_U, t, rows, :] = up_u
            flat[LO_U, t, rows, :] = lo_u
            flat[UP_V, t, rows, :] = up_v
            flat[C_U, t, rows, :] = count_u * (-substep_time * layer)
            flat[C_V, t, rows, :] = count_v * (-substep_time * layer)
            flat[F_U, t, rows, :] = jnp.where(count_u > 0.0, substep_time * ft_ref[rows, :], 0.0)
            flat[F_V, t, rows, :] = jnp.where(count_v > 0.0, -substep_time * fv_ref[rows, :], 0.0)
            flat[SEA, t, rows, :] = jnp.where(bed[t] > 0.0, substep_time, 0.0)

    def mask_at(r, k):
        rows = pl.ds(pl.multiple_of(r * 8, 8) + PAD, 8)
        mu = [(flat[LO_U, t, rows, :] <= k) & (flat[UP_U, t, rows, :] > k) for t in range(2)]
        mv = [(flat[FROM, t, rows, :] <= k) & (flat[UP_V, t, rows, :] > k) for t in range(2)]
        return mu, mv

    def mask_first(r, carry):
        rows = pl.ds(pl.multiple_of(r * 8, 8) + PAD, 8)
        for t in range(2):
            lo_u, up_u = flat[LO_U, t, rows, :], flat[UP_U, t, rows, :]
            lo_v, up_v = flat[FROM, t, rows, :], flat[UP_V, t, rows, :]
            sum_u = jnp.zeros((8, LANES), jnp.float32)
            sum_v = jnp.zeros((8, LANES), jnp.float32)
            for k in range(LEVELS):
                u = jnp.where((lo_u <= k) & (up_u > k), u_all[k, t, rows, :], 0.0)
                v = jnp.where((lo_v <= k) & (up_v > k), v_all[k, t, rows, :], 0.0)
                u_all[k, t, rows, :] = u
                v_all[k, t, rows, :] = v
                sum_u = sum_u + u
                sum_v = sum_v + v
            flow_u[0, t, rows, :] = layer * sum_u
            flow_v[0, t, rows, :] = layer * sum_v
        return carry

    for flow in (flow_u, flow_v):
        for now in range(2):
            for t in range(2):
                flow[now, t, pl.ds(0, PAD), :] = jnp.zeros((PAD, LANES), jnp.float32)
                flow[now, t, pl.ds(PAD + EXT, PAD), :] = jnp.zeros((PAD, LANES), jnp.float32)

    lax.fori_loop(0, EXT // 8, mask_first, 0)

    for step in range(STEPS):
        for k in range(LEVELS):
            fold_ghosts(u_all.at[k], top)
            fold_ghosts(v_all.at[k], top, -1.0)
            if step == 0:
                fold_ghosts(p_all.at[k], top)
        fold_ghosts(flow_u.at[0], top)

        def tendencies(r, carry):
            base = pl.multiple_of(r * 8, 8) + PAD
            rows, up, down = pl.ds(base, 8), pl.ds(base + 1, 8), pl.ds(base - 1, 8)
            ft, fv = ft_ref[rows, :], fv_ref[rows, :]
            lo_u = [flat[LO_U, t, rows, :] for t in range(2)]
            up_u = [flat[UP_U, t, rows, :] for t in range(2)]
            lo_v = [flat[FROM, t, rows, :] for t in range(2)]
            up_v = [flat[UP_V, t, rows, :] for t in range(2)]
            zero = jnp.zeros((8, LANES), jnp.float32)
            force_u, force_v, total_u, total_v = [zero] * 2, [zero] * 2, [zero] * 2, [zero] * 2
            for k in range(LEVELS):
                eu, wu, ru, ev, wv, rv, u0s, v0s = [], [], [], [], [], [], [], []
                for t in range(2):
                    u0, un, us = u_all[k, t, rows, :], u_all[k, t, up, :], u_all[k, t, down, :]
                    v0, vn, vs = v_all[k, t, rows, :], v_all[k, t, up, :], v_all[k, t, down, :]
                    p0, pn = p_all[k, t, rows, :], p_all[k, t, up, :]
                    turn_v = ft * (v0 + vs)
                    turn_u = fv * (u0 + un)
                    a = viscosity * u0
                    c = viscosity * v0
                    eu.append(a - p0 + turn_v)
                    wu.append(a)
                    ru.append(viscosity * (un + us) - 4.0 * a + p0 + turn_v)
                    ev.append(c)
                    wv.append(c - turn_u)
                    rv.append(viscosity * (vn + vs) - 4.0 * c + (p0 - pn) - turn_u)
                    u0s.append(u0)
                    v0s.append(v0)
                eu, wu, ev, wv = eastward(*eu), westward(*wu), eastward(*ev), westward(*wv)
                for t in range(2):
                    tend_u = jnp.where((lo_u[t] <= k) & (up_u[t] > k), eu[t] + wu[t] + ru[t], 0.0)
                    tend_v = jnp.where((lo_v[t] <= k) & (up_v[t] > k), ev[t] + wv[t] + rv[t], 0.0)
                    force_u[t] = force_u[t] + tend_u
                    force_v[t] = force_v[t] + tend_v
                    new_u = u0s[t] + step_time * tend_u
                    new_v = v0s[t] + step_time * tend_v
                    new_u = jnp.where(up_u[t] == k + 1, drag * new_u, new_u)
                    new_v = jnp.where(up_v[t] == k + 1, drag * new_v, new_v)
                    total_u[t] = total_u[t] + new_u
                    total_v[t] = total_v[t] + new_v
                    u_new[k, t, rows, :] = new_u
                    v_new[k, t, rows, :] = new_v
            for t in range(2):
                flat[G_U, t, rows, :] = (substep_time * layer) * force_u[t]
                flat[G_V, t, rows, :] = (substep_time * layer) * force_v[t]
                flat[NEW_U, t, rows, :] = layer * total_u[t]
                flat[NEW_V, t, rows, :] = layer * total_v[t]
                flat[SUM_U, t, rows, :] = zero
                flat[SUM_V, t, rows, :] = zero
            return carry

        lax.fori_loop(0, EXT // 8, tendencies, 0)

        def substep(now, later):
            for at, n in CHUNKS:
                rows, down = pl.ds(PAD + at, n), pl.ds(PAD + at - 1, n)
                u = [flow_u[now, t, rows, :] for t in range(2)]
                uw = westward(*u)
                for t in range(2):
                    spread = u[t] - uw[t] + flow_v[now, t, rows, :] - flow_v[now, t, down, :]
                    height[t, rows, :] = height[t, rows, :] - flat[SEA, t, rows, :] * spread
            fold_ghosts(height, top)
            for at, n in CHUNKS:
                rows, up, down = pl.ds(PAD + at, n), pl.ds(PAD + at + 1, n), pl.ds(PAD + at - 1, n)
                h = [height[t, rows, :] for t in range(2)]
                he = eastward(*h)
                qv = [flow_v[now, t, rows, :] + flow_v[now, t, down, :] for t in range(2)]
                qve = eastward(*qv)
                qu = [flow_u[now, t, rows, :] + flow_u[now, t, up, :] for t in range(2)]
                quw = westward(*qu)
                for t in range(2):
                    next_u = (
                        flow_u[now, t, rows, :]
                        + flat[C_U, t, rows, :] * (he[t] - h[t])
                        + flat[F_U, t, rows, :] * (qv[t] + qve[t])
                        + flat[G_U, t, rows, :]
                    )
                    next_v = (
                        flow_v[now, t, rows, :]
                        + flat[C_V, t, rows, :] * (height[t, up, :] - h[t])
                        + flat[F_V, t, rows, :] * (qu[t] + quw[t])
                        + flat[G_V, t, rows, :]
                    )
                    flow_u[later, t, rows, :] = next_u
                    flow_v[later, t, rows, :] = next_v
                    flat[SUM_U, t, rows, :] = flat[SUM_U, t, rows, :] + next_u
                    flat[SUM_V, t, rows, :] = flat[SUM_V, t, rows, :] + next_v
            fold_ghosts(flow_u.at[later], top)

        def two_substeps(turn, carry):
            substep(0, 1)
            substep(1, 0)
            return carry

        lax.fori_loop(0, SUBSTEPS // 2, two_substeps, 0)

        last = step == STEPS - 1

        def correct(r, carry):
            base = pl.multiple_of(r * 8, 8) + PAD
            rows = pl.ds(base, 8)
            for t in range(1 if last else 2):
                lo_u, up_u = flat[LO_U, t, rows, :], flat[UP_U, t, rows, :]
                lo_v, up_v = flat[FROM, t, rows, :], flat[UP_V, t, rows, :]
                mean_u = flat[SUM_U, t, rows, :] / SUBSTEPS
                mean_v = flat[SUM_V, t, rows, :] / SUBSTEPS
                depth_u = layer * jnp.maximum(up_u - lo_u, 1.0)
                depth_v = layer * jnp.maximum(up_v - lo_v, 1.0)
                add_u = (mean_u - flat[NEW_U, t, rows, :]) / depth_u
                add_v = (mean_v - flat[NEW_V, t, rows, :]) / depth_v
                for k in range(LEVELS):
                    u = jnp.where((lo_u <= k) & (up_u > k), u_new[k, t, rows, :] + add_u, 0.0)
                    v = jnp.where((lo_v <= k) & (up_v > k), v_new[k, t, rows, :] + add_v, 0.0)
                    if last:
                        out = pl.ds(pl.multiple_of(r * 8 - OWN, 8), 8)
                        u_out[k, out, :] = u
                        v_out[k, out, :] = v
                    else:
                        u_all[k, t, rows, :] = u
                        v_all[k, t, rows, :] = v
                if not last:
                    flow_u[0, t, rows, :] = mean_u
                    flow_v[0, t, rows, :] = mean_v
            return carry

        if last:
            lax.fori_loop(OWN // 8, (OWN + ROWS) // 8, correct, 0)
        else:
            lax.fori_loop(0, EXT // 8, correct, 0)

    h_out[...] = height[0, pl.ds(PAD + OWN, ROWS), :]


def lon_swaps():
    count = lax.axis_size("lon")
    first = [(i, i ^ 1) for i in range(count)]
    second = [(i, (((i + 1) % count) ^ 1) - 1) for i in range(count)]
    return first, [(i, j % count) for i, j in second]


def lat_swaps():
    lats, lons = lax.axis_size("lat"), lax.axis_size("lon")
    first, second = [], []
    for lat in range(lats):
        for lon in range(lons):
            first.append((lon * lats + lat, lon * lats + (lat ^ 1)))
            if lat == lats - 1:
                second.append((lon * lats + lat, (lons - 1 - lon) * lats + lat))
            elif lat:
                second.append((lon * lats + lat, lon * lats + ((lat + 1) ^ 1) - 1))
    return first, second


def turning(lat):
    lats = lax.axis_size("lat")
    ext = jnp.arange(TALL, dtype=jnp.int32) - PAD
    mirror = (lat == lats - 1) & (ext >= PATCH)
    row = jnp.where(mirror, lats * ROWS - FOLD + ext - PATCH, lat * ROWS + ext - OWN).astype(jnp.float32)
    sign = jnp.where(mirror, -0.25 * coriolis, 0.25 * coriolis)
    cells = lats * ROWS
    centre = sign * jnp.sin(math.pi * ((row + 0.5) / cells - 0.5))
    face = sign * jnp.sin(math.pi * ((row + 1.0) / cells - 0.5))
    wide = (TALL, LANES)
    return jnp.broadcast_to(centre[:, None], wide), jnp.broadcast_to(face[:, None], wide)


def whole(*shape):
    return pl.BlockSpec(shape, lambda *_: (0,) * len(shape))


def shards(u_velocity, v_velocity, density, surface, land_mask, bottom):
    f32 = jnp.float32
    params = pltpu.CompilerParams(vmem_limit_bytes=VMEM_LIMIT)
    level_block = (LEVELS, ROWS, LANES)
    own, pack_a, pack_b = pl.pallas_call(
        prepare,
        out_shape=(
            jax.ShapeDtypeStruct((PLANES, ROWS, LANES), f32),
            jax.ShapeDtypeStruct((PACKS, ROWS, LANES), f32),
            jax.ShapeDtypeStruct((PACKS, ROWS, LANES), f32),
        ),
        compiler_params=params,
    )(u_velocity, v_velocity, density, surface, land_mask, bottom)
    lon_first, lon_second = lon_swaps()
    east_a = lax.ppermute(pack_a, "lon", lon_first)
    east_b = lax.ppermute(pack_b, "lon", lon_second)

    low = lambda planes: pl.BlockSpec((planes, 24, LANES), lambda i: (0, 0, 0))
    high = lambda planes: pl.BlockSpec((planes, 24, LANES), lambda i: (0, ROWS // 24 - 1, 0))
    rows_a, rows_b = pl.pallas_call(
        outer_rows,
        grid=(1,),
        in_specs=[low(PLANES), low(PACKS), low(PACKS), high(PLANES), high(PACKS), high(PACKS)],
        out_specs=(whole(SENT * HALO, LANES), whole(888, LANES)),
        out_shape=(
            jax.ShapeDtypeStruct((SENT * HALO, LANES), f32),
            jax.ShapeDtypeStruct((888, LANES), f32),
        ),
        compiler_params=params,
    )(own, east_a, east_b, own, east_a, east_b)
    lat_first, lat_second = lat_swaps()
    north_a = lax.ppermute(rows_a, ("lon", "lat"), lat_first)
    north_b = lax.ppermute(rows_b, ("lon", "lat"), lat_second)

    turn_centre, turn_face = turning(lax.axis_index("lat"))
    levels_scratch = pltpu.VMEM((LEVELS, 2, TALL, LANES), f32)
    return pl.pallas_call(
        ocean_steps,
        out_shape=(
            jax.ShapeDtypeStruct(level_block, f32),
            jax.ShapeDtypeStruct(level_block, f32),
            jax.ShapeDtypeStruct((ROWS, LANES), f32),
        ),
        scratch_shapes=[levels_scratch] * 5
        + [
            pltpu.VMEM((16, 2, TALL, LANES), f32),
            pltpu.VMEM((2, 2, TALL, LANES), f32),
            pltpu.VMEM((2, 2, TALL, LANES), f32),
            pltpu.VMEM((2, TALL, LANES), f32),
        ],
        compiler_params=params,
    )(own, east_a, east_b, north_a, north_b, turn_centre, turn_face)


def solution(mesh):
    return jax.shard_map(
        shards,
        mesh=mesh,
        in_specs=(
            P(None, "lat", "lon"),
            P(None, "lat", "lon"),
            P(None, "lat", "lon"),
            P("lat", "lon"),
            P(None, "lat", "lon"),
            P("lat", "lon"),
        ),
        out_specs=(P(None, "lat", "lon"), P(None, "lat", "lon"), P("lat", "lon")),
        check_vma=False,
    )
```

time: 1130 us -> 61.4 us (0.05); the launches traced: 1110 us -> 60.6 us
  waiting for transfers between devices: 508 us -> 21.5 us
  starting transfers between devices: 497 us -> 12.8 us
  other arithmetic: 63.7 us -> 0.06 us
  local copies, waits for them, and re-layouts: 35.6 us -> 2.24 us
  Pallas kernels: 0 us -> 23.4 us
    ppermute x280 -> x4, waiting for transfers between devices: 508 us -> 21.5 us  [the longest x1 14 us: shards(): north_b = lax.ppermute(rows_b, ('lon', 'lat'), lat_second)]
    ppermute x280 -> x4, starting transfers between devices: 497 us -> 12.8 us  [the longest x1 7.3 us: shards(): east_b = lax.ppermute(pack_b, 'lon', lon_second)]
    pallas_call x0 -> x3, Pallas kernels: none -> 23.4 us  [the longest x1 17.3 us: shards(): pl.pallas_call(ocean_steps, out_shape=(jax.ShapeDtypeStruct(level_block,...]
    reduce_sum x3 -> x0, other arithmetic: 13.1 us -> none  [the longest x2 9.86 us: shards(): jnp.sum(new_v, axis=0)]
    slice x56 -> x0, local copies, waits for them, and re-layouts: 11.4 us -> none  [the longest x20 6.91 us: extended(): lax.slice_in_dim(cells, cells.shape[dim] - width, cells.shape[dim], axis=...]
  transfers between devices with their start and end apart: 280 -> 4, of which waited for: 175 -> 3; matrix products, arithmetic and copies ran while one was open for 2% -> 0% of each run, Pallas kernels for 0% -> 0%
where the time goes in v1:
time: 61.4 us; the launch traced here: 60.6 us
  Pallas kernels  23.4 us (38%)
  waiting for transfers between devices  21.5 us (35%)
  starting transfers between devices  12.8 us (21%)
  local copies, waits for them, and re-layouts  2.24 us (4%)
  between operations  0.67 us (1%)
    pallas_call x1, Pallas kernels, shards(): pl.pallas_call(ocean_steps, out_shape=(jax.ShapeDtypeStruct(level_block,...  17.3 us
    ppermute x1, waiting for transfers between devices, shards(): north_b = lax.ppermute(rows_b, ('lon', 'lat'), lat_second)  14 us
    ppermute x1, starting transfers between devices, shards(): east_b = lax.ppermute(pack_b, 'lon', lon_second)  7.3 us
    ppermute x1, waiting for transfers between devices, shards(): east_b = lax.ppermute(pack_b, 'lon', lon_second)  5.56 us
    pallas_call x1, Pallas kernels, shards(): pl.pallas_call(prepare, out_shape=(jax.ShapeDtypeStruct((PLANES, ROWS, LA...  3.91 us
    ppermute x1, starting transfers between devices, shards(): north_b = lax.ppermute(rows_b, ('lon', 'lat'), lat_second)  3.73 us
    pallas_call x1, Pallas kernels, shards(): pl.pallas_call(outer_rows, grid=(1,), in_specs=[low(PLANES), low(PACKS),...  2.2 us
    ppermute x1, waiting for transfers between devices, shards(): north_a = lax.ppermute(rows_a, ('lon', 'lat'), lat_first)  1.86 us
  transfers between devices with their start and end apart: 4, of which 3 were waited for; matrix products, arithmetic and copies ran while one was open for 0% of the time, Pallas kernels for 0%

profile of v1, /device:TPU:7, one launch (start us, length us, event | category | flops | bytes accessed | tf_op | source)
XLA Modules:
  0.0 60.6 jit_solution(8165349421127298707)
XLA Ops:
  0.6 3.9 %shard_map.85 = (f32[39,96,128]{2,1,0:T(8,128)}, f32[5,96,128]{2,1,0:T(8,128)}, f32[5,96,128]{2,1,0:T(8,128)}) custom-call(f32[12,96,128]{2,1,0:T(8,128)} %u_ref.1, f32[12,96,128]{2,1,0:T(8,128)} %v_ref.1, f32[12,96,128]{2,1,0:T(8,128)} %d_ref.1, f32[96,128]{1,0:T(8,128)} %s_ref.1, s32[12,96,128]{2,1,0:T(8,128)} %m_ref.1, s32[96,128]{1,0:T(8,128)} %b_ref.1), custom_call_target="tpu_custom_call" | custom-call | tf_op jit(solution)/shard_map/pallas_call | solution.py:433
  4.5 1.6 %collective-permute-start = (f32[5,96,128]{2,1,0:T(8,128)}, f32[5,96,128]{2,1,0:T(8,128)S(1)}, u32[]{:S(2)}, u32[]{:S(2)}) collective-permute-start(f32[5,96,128]{2,1,0:T(8,128)} %get-tuple-element.9), channel_id=1, source_target_pairs={{0,16},{16,0},{32,48},{48,32},{64,80},{80,64},{96,112},{112,96},{1... | collective-permute-start | bytes 737288 | tf_op jit(solution)/shard_map/ppermute | solution.py:443
  6.2 7.3 %collective-permute-start.1 = (f32[5,96,128]{2,1,0:T(8,128)}, f32[5,96,128]{2,1,0:T(8,128)S(1)}, u32[]{:S(2)}, u32[]{:S(2)}) collective-permute-start(f32[5,96,128]{2,1,0:T(8,128)} %get-tuple-element.10), channel_id=1, source_target_pairs={{0,240},{16,32},{32,16},{48,64},{64,48},{80,96},{96,80},{112,128},... | collective-permute-start | bytes 737288 | tf_op jit(solution)/shard_map/ppermute | solution.py:444
  13.5 0.0 collective-permute-done.low_a.top_a.ea_ref
  13.5 0.0 copy-start
  13.5 5.6 %collective-permute-done.1.low_b.top_b.eb_ref = f32[5,96,128]{2,1,0:T(8,128)S(1)} collective-permute-done((f32[5,96,128]{2,1,0:T(8,128)}, f32[5,96,128]{2,1,0:T(8,128)S(1)}, u32[]{:S(2)}, u32[]{:S(2)}) %collective-permute-start.1) | collective-permute-done | bytes 245792 | tf_op jit(solution)/shard_map/ppermute | solution.py:444
  19.0 0.0 copy-start.1
  19.0 0.0 copy-done
  19.0 0.7 %copy-done.1 = f32[5,96,128]{2,1,0:T(8,128)} copy-done((f32[5,96,128]{2,1,0:T(8,128)}, f32[5,96,128]{2,1,0:T(8,128)S(1)}, u32[]{:S(2)}) %copy-start.1) | copy-done | bytes 245784
  19.7 2.2 %shard_map.86 = (f32[784,128]{1,0:T(8,128)}, f32[888,128]{1,0:T(8,128)}) custom-call(f32[39,96,128]{2,1,0:T(8,128)} %get-tuple-element.8.low_own.top_own.own_ref, f32[5,96,128]{2,1,0:T(8,128)} %copy-done, f32[5,96,128]{2,1,0:T(8,128)} %copy-done.1, f32[39,96,128]{2,1,0:T(8,128)} %get-tuple-element.8.low_own.top_own.own_ref, f32[5,96,128]{2,1,0:T(8,128)} %copy-done, ...), custom_call_target="tpu_custom_call" | custom-call | tf_op jit(solution)/shard_map/pallas_call | solution.py:448
  21.9 3.7 %collective-permute-start.3 = (f32[888,128]{1,0:T(8,128)}, f32[888,128]{1,0:T(8,128)S(1)}, u32[]{:S(2)}, u32[]{:S(2)}) collective-permute-start(f32[888,128]{1,0:T(8,128)} %get-tuple-element.12), channel_id=1, source_target_pairs={{1,2},{17,18},{33,34},{49,50},{65,66},{81,82},{97,98},{113,114},{1... | collective-permute-start | bytes 1363976 | tf_op jit(solution)/shard_map/ppermute | solution.py:461
  25.7 0.1 collective-permute-start.2
  25.8 0.1 select_multiply_fusion
  25.8 1.9 %collective-permute-done.2.na_ref = f32[784,128]{1,0:T(8,128)S(1)} collective-permute-done((f32[784,128]{1,0:T(8,128)}, f32[784,128]{1,0:T(8,128)S(1)}, u32[]{:S(2)}, u32[]{:S(2)}) %collective-permute-start.2) | collective-permute-done | bytes 401440 | tf_op jit(solution)/shard_map/ppermute | solution.py:460
  27.7 0.0 copy-start.3
  27.7 14.0 %collective-permute-done.3.nb_ref = f32[888,128]{1,0:T(8,128)S(1)} collective-permute-done((f32[888,128]{1,0:T(8,128)}, f32[888,128]{1,0:T(8,128)S(1)}, u32[]{:S(2)}, u32[]{:S(2)}) %collective-permute-start.3) | collective-permute-done | bytes 454688 | tf_op jit(solution)/shard_map/ppermute | solution.py:461
  41.7 0.0 copy-start.2
  41.7 0.8 %broadcast_in_dim.23.fv_ref = f32[152,128]{1,0:T(8,128)} broadcast(f32[152]{0:T(256)S(1)} %get-tuple-element.13), dimensions={0} | broadcast | bytes 78432 | tf_op jit(solution)/shard_map/broadcast_in_dim | solution.py:422
  42.5 0.7 %broadcast_in_dim.22.ft_ref = f32[152,128]{1,0:T(8,128)} broadcast(f32[152]{0:T(256)S(1)} %get-tuple-element.14), dimensions={0} | broadcast | bytes 78432 | tf_op jit(solution)/shard_map/broadcast_in_dim | solution.py:422
  43.3 0.0 copy-done.3
  43.3 0.0 copy-done.2
  43.3 17.3 %shard_map.87 = (f32[12,96,128]{2,1,0:T(8,128)}, f32[12,96,128]{2,1,0:T(8,128)}, f32[96,128]{1,0:T(8,128)}) custom-call(f32[39,96,128]{2,1,0:T(8,128)} %get-tuple-element.8.low_own.top_own.own_ref, f32[5,96,128]{2,1,0:T(8,128)} %copy-done, f32[5,96,128]{2,1,0:T(8,128)} %copy-done.1, f32[784,128]{1,0:T(8,128)} %copy-done.3, f32[888,128]{1,0:T(8,128)} %copy-done.2, ...), custom_call_target="tpu_custom_call" | custom-call | tf_op jit(solution)/shard_map/pallas_call | solution.py:465
Async XLA Ops:
  4.5 8.9 %collective-permute-start = (f32[5,96,128]{2,1,0:T(8,128)}, f32[5,96,128]{2,1,0:T(8,128)S(1)}, u32[]{:S(2)}, u32[]{:S(2)}) collective-permute-start(f32[5,96,128]{2,1,0:T(8,128)} %get-tuple-element.9), channel_id=1, source_target_pairs={{0,16},{16,0},{32,48},{48,32},{64,80},{80,64},{96,112},{112,96},{1... | collective-permute-start | bytes 737288 | tf_op jit(solution)/shard_map/ppermute | solution.py:443
  6.2 12.9 %collective-permute-start.1 = (f32[5,96,128]{2,1,0:T(8,128)}, f32[5,96,128]{2,1,0:T(8,128)S(1)}, u32[]{:S(2)}, u32[]{:S(2)}) collective-permute-start(f32[5,96,128]{2,1,0:T(8,128)} %get-tuple-element.10), channel_id=1, source_target_pairs={{0,240},{16,32},{32,16},{48,64},{64,48},{80,96},{96,80},{112,128},... | collective-permute-start | bytes 737288 | tf_op jit(solution)/shard_map/ppermute | solution.py:444
  13.5 5.6 %copy-start = (f32[5,96,128]{2,1,0:T(8,128)}, f32[5,96,128]{2,1,0:T(8,128)S(1)}, u32[]{:S(2)}) copy-start(f32[5,96,128]{2,1,0:T(8,128)S(1)} %collective-permute-done.low_a.top_a.ea_ref) | copy-start | bytes 737284
  19.0 0.7 %copy-start.1 = (f32[5,96,128]{2,1,0:T(8,128)}, f32[5,96,128]{2,1,0:T(8,128)S(1)}, u32[]{:S(2)}) copy-start(f32[5,96,128]{2,1,0:T(8,128)S(1)} %collective-permute-done.1.low_b.top_b.eb_ref) | copy-start | bytes 737284
  21.9 19.8 %collective-permute-start.3 = (f32[888,128]{1,0:T(8,128)}, f32[888,128]{1,0:T(8,128)S(1)}, u32[]{:S(2)}, u32[]{:S(2)}) collective-permute-start(f32[888,128]{1,0:T(8,128)} %get-tuple-element.12), channel_id=1, source_target_pairs={{1,2},{17,18},{33,34},{49,50},{65,66},{81,82},{97,98},{113,114},{1... | collective-permute-start | bytes 1363976 | tf_op jit(solution)/shard_map/ppermute | solution.py:461
  25.7 2.0 %collective-permute-start.2 = (f32[784,128]{1,0:T(8,128)}, f32[784,128]{1,0:T(8,128)S(1)}, u32[]{:S(2)}, u32[]{:S(2)}) collective-permute-start(f32[784,128]{1,0:T(8,128)} %get-tuple-element.11), channel_id=1, source_target_pairs={{0,1},{16,17},{32,33},{48,49},{64,65},{80,81},{96,97},{112,113},{1... | collective-permute-start | bytes 1204232 | tf_op jit(solution)/shard_map/ppermute | solution.py:460
  27.7 15.6 %copy-start.3 = (f32[784,128]{1,0:T(8,128)}, f32[784,128]{1,0:T(8,128)S(1)}, u32[]{:S(2)}) copy-start(f32[784,128]{1,0:T(8,128)S(1)} %collective-permute-done.2.na_ref) | copy-start | bytes 1204228
  41.7 1.6 %copy-start.2 = (f32[888,128]{1,0:T(8,128)}, f32[888,128]{1,0:T(8,128)S(1)}, u32[]{:S(2)}) copy-start(f32[888,128]{1,0:T(8,128)S(1)} %collective-permute-done.3.nb_ref) | copy-start | bytes 1363972

commit v2 on v1

v2 whole, which is shorter than its diff:
```python
import math

import jax
import jax.numpy as jnp
from jax import lax
from jax.experimental import pallas as pl
from jax.experimental.pallas import tpu as pltpu
from jax.sharding import PartitionSpec as P

SUBSTEPS = 8
STEPS = 2
LEVELS = 12
ROWS = 96
LANES = 128
HALO = 16
FOLD = 18

PLANES = 3 * LEVELS + 3
BOTTOM, FIRST, SURFACE = 36, 37, 38
PACKS = -(-PLANES // 8)
SENT = PLANES + 2 * PACKS

PAD = 8
EXT = 136
TALL = PAD + EXT + PAD
OWN = HALO
GHOST_A, PATCH, GHOST_B = OWN + ROWS, OWN + ROWS + 1, OWN + ROWS + 1 + FOLD
CHUNKS = ((0, 32), (32, 32), (64, 32), (96, 40))

viscosity = 0.05
friction = 0.1
coriolis = 0.25
substep_time = 0.4
layer = 1.0 / LEVELS
step_time = SUBSTEPS * substep_time
drag = 1.0 / (1.0 + step_time * friction)

VMEM_LIMIT = 24 * 1024 * 1024


def lanes_of(shape):
    return lax.broadcasted_iota(jnp.int32, shape, len(shape) - 1)


def masked_planes(u_ref, v_ref, d_ref, s_ref, m_ref, b_ref, ready):
    lane = lanes_of((ROWS, LANES))
    row = lax.broadcasted_iota(jnp.int32, (ROWS, LANES), 0)
    ready(5)
    ready(4)
    bottom = b_ref[...].astype(jnp.float32)
    first = bottom - jnp.sum(m_ref[...], axis=0).astype(jnp.float32)
    east = jnp.where(lane == LANES - 1, 12.0, pltpu.roll(bottom, LANES - 1, 1))
    north = jnp.where(row == ROWS - 1, 12.0, pltpu.roll(bottom, ROWS - 1, 0))
    up_u, up_v = jnp.minimum(bottom, east), jnp.minimum(bottom, north)
    ready(0)
    for k in range(LEVELS):
        yield k, jnp.where((first <= k) & (up_u > k), u_ref[k], 0.0)
    ready(1)
    for k in range(LEVELS):
        yield LEVELS + k, jnp.where((first <= k) & (up_v > k), v_ref[k], 0.0)
    ready(2)
    running = jnp.zeros_like(bottom)
    for k in range(LEVELS):
        weighted = jnp.where((first <= k) & (bottom > k), d_ref[k], 0.0)
        running = running + weighted
        yield 2 * LEVELS + k, layer * (running - 0.5 * weighted)
    ready(3)
    yield BOTTOM, bottom
    yield FIRST, first
    yield SURFACE, jnp.where(bottom > 0.0, s_ref[...], 0.0)


def strips(u_far, v_far, d_far, s_far, m_far, b_far, a_ref, c_ref, u_ref, v_ref, d_ref, s_ref, m_ref, b_ref, sems):
    pairs = ((u_far, u_ref), (v_far, v_ref), (d_far, d_ref), (s_far, s_ref), (m_far, m_ref), (b_far, b_ref))
    copies = [pltpu.make_async_copy(far, near, sems.at[i]) for i, (far, near) in enumerate(pairs)]
    for i in (5, 4, 0, 1, 2, 3):
        copies[i].start()
    lane = lanes_of((ROWS, LANES))
    even = lax.rem(lax.axis_index("lon"), 2) == 0
    for p, plane in masked_planes(u_ref, v_ref, d_ref, s_ref, m_ref, b_ref, lambda i: copies[i].wait()):
        slot = p % 8
        here = (lane >= HALO * slot) & (lane < HALO * slot + HALO)
        if slot == 0:
            to_east = to_west = jnp.zeros((ROWS, LANES), jnp.float32)
        to_east = jnp.where(here, pltpu.roll(plane, (HALO * slot + HALO) % LANES, 1), to_east)
        to_west = jnp.where(here, pltpu.roll(plane, HALO * slot, 1) if slot else plane, to_west)
        if slot == 7 or p == PLANES - 1:
            a_ref[p // 8] = jnp.where(even, to_east, to_west)
            c_ref[p // 8] = jnp.where(even, to_west, to_east)


def own_block(u_ref, v_ref, d_ref, s_ref, m_ref, b_ref, own_ref):
    for p, plane in masked_planes(u_ref, v_ref, d_ref, s_ref, m_ref, b_ref, lambda i: None):
        own_ref[p] = plane


def outer_rows(low_own, low_a, low_b, top_own, top_a, top_b, a_ref, c_ref):
    even = lax.rem(lax.axis_index("lat"), 2) == 0
    for p in range(SENT):
        if p < PLANES:
            low, top = low_own[p], top_own[p]
        elif p < PLANES + PACKS:
            low, top = low_a[p - PLANES], top_a[p - PLANES]
        else:
            low, top = low_b[p - PLANES - PACKS], top_b[p - PLANES - PACKS]
        a_ref[pl.ds(p * HALO, HALO), :] = jnp.where(even, top[24 - HALO :], low[:HALO])
        c_ref[pl.ds(p * FOLD, FOLD), :] = jnp.where(even, low[:FOLD], top[24 - FOLD :])


def eastward(t0, t1):
    lane = lanes_of(t0.shape)
    r0, r1 = pltpu.roll(t0, LANES - 1, t0.ndim - 1), pltpu.roll(t1, LANES - 1, t0.ndim - 1)
    edge = lane == LANES - 1
    return jnp.where(edge, r1, r0), jnp.where(edge, r0, r1)


def westward(t0, t1):
    lane = lanes_of(t0.shape)
    r0, r1 = pltpu.roll(t0, 1, t0.ndim - 1), pltpu.roll(t1, 1, t0.ndim - 1)
    edge = lane == 0
    return jnp.where(edge, r1, r0), jnp.where(edge, r0, r1)


def fold_ghosts(ref, top, sign=1.0):
    for t in range(2):
        for ghost, source in ((GHOST_A, PATCH + FOLD - 2), (GHOST_B, OWN + ROWS - 2)):
            kept = ref[t, pl.ds(PAD + ghost, 1), :]
            taken = ref[t, pl.ds(PAD + source, 1), :]
            ref[t, pl.ds(PAD + ghost, 1), :] = jnp.where(top, sign * taken, kept)


(BED, FROM, UP_U, LO_U, UP_V, C_U, F_U, G_U, C_V, F_V, G_V, SUM_U, SUM_V, NEW_U, NEW_V, SEA) = range(16)
INNER = (3, 12)
SUMS = (G_U, G_V, NEW_U, NEW_V)


def beyond(p):
    return 12.0 if p in (BOTTOM, FIRST) else 0.0


def beside(east, west, p):
    lane = lanes_of(east.shape)
    slot = HALO * (p % 8)
    e = pltpu.roll(east, LANES - slot, 1) if slot else east
    w = pltpu.roll(west, (2 * LANES - HALO - slot) % LANES, 1) if slot != LANES - HALO else west
    return jnp.where(lane < HALO, e, jnp.where(lane >= LANES - HALO, w, beyond(p)))


def planes_of(pack):
    return range(8 * pack, min(8 * pack + 8, PLANES))


def faces(at, n, flat, ft_ref, fv_ref, top):
    rows, up = pl.ds(PAD + at, n), pl.ds(PAD + at + 1, n)
    bed = [flat[BED, t, rows, :] for t in range(2)]
    start = [flat[FROM, t, rows, :] for t in range(2)]
    bed_east = eastward(*bed)
    start_east = eastward(*start)
    ext_row = lax.broadcasted_iota(jnp.int32, (n, LANES), 0) + at
    mirror = (ext_row >= jnp.where(top, PATCH, EXT)) & (ext_row < PATCH + FOLD)
    for t in range(2):
        up_u = jnp.minimum(bed[t], bed_east[t])
        lo_u = jnp.where(mirror, start_east[t], start[t])
        up_v = jnp.minimum(bed[t], flat[BED, t, up, :])
        count_u = jnp.maximum(up_u - lo_u, 0.0)
        count_v = jnp.maximum(up_v - start[t], 0.0)
        flat[UP_U, t, rows, :] = up_u
        flat[LO_U, t, rows, :] = lo_u
        flat[UP_V, t, rows, :] = up_v
        flat[C_U, t, rows, :] = count_u * (-substep_time * layer)
        flat[C_V, t, rows, :] = count_v * (-substep_time * layer)
        flat[F_U, t, rows, :] = jnp.where(count_u > 0.0, substep_time * ft_ref[rows, :], 0.0)
        flat[F_V, t, rows, :] = jnp.where(count_v > 0.0, -substep_time * fv_ref[rows, :], 0.0)
        flat[SEA, t, rows, :] = jnp.where(bed[t] > 0.0, substep_time, 0.0)


def mask_rows(r, flat, u_all, v_all, flow_u, flow_v):
    rows = pl.ds(pl.multiple_of(r * 8, 8) + PAD, 8)
    for t in range(2):
        lo_u, up_u = flat[LO_U, t, rows, :], flat[UP_U, t, rows, :]
        lo_v, up_v = flat[FROM, t, rows, :], flat[UP_V, t, rows, :]
        us = [jnp.where((lo_u <= k) & (up_u > k), u_all[k, t, rows, :], 0.0) for k in range(LEVELS)]
        vs = [jnp.where((lo_v <= k) & (up_v > k), v_all[k, t, rows, :], 0.0) for k in range(LEVELS)]
        for k in range(LEVELS):
            u_all[k, t, rows, :] = us[k]
            v_all[k, t, rows, :] = vs[k]
        flow_u[0, t, rows, :] = layer * sum(us[1:], us[0])
        flow_v[0, t, rows, :] = layer * sum(vs[1:], vs[0])


def tendencies(r, flat, ft_ref, fv_ref, u_all, v_all, p_all, u_new, v_new):
    base = pl.multiple_of(r * 8, 8) + PAD
    rows, up, down = pl.ds(base, 8), pl.ds(base + 1, 8), pl.ds(base - 1, 8)
    ft, fv = ft_ref[rows, :], fv_ref[rows, :]
    lo_u = [flat[LO_U, t, rows, :] for t in range(2)]
    up_u = [flat[UP_U, t, rows, :] for t in range(2)]
    lo_v = [flat[FROM, t, rows, :] for t in range(2)]
    up_v = [flat[UP_V, t, rows, :] for t in range(2)]
    zero = jnp.zeros((8, LANES), jnp.float32)
    force_u, force_v, total_u, total_v = [zero] * 2, [zero] * 2, [zero] * 2, [zero] * 2
    for k in range(LEVELS):
        eu, wu, ru, ev, wv, rv, u0s, v0s = [], [], [], [], [], [], [], []
        for t in range(2):
            u0, un, us = u_all[k, t, rows, :], u_all[k, t, up, :], u_all[k, t, down, :]
            v0, vn, vs = v_all[k, t, rows, :], v_all[k, t, up, :], v_all[k, t, down, :]
            p0, pn = p_all[k, t, rows, :], p_all[k, t, up, :]
            turn_v = ft * (v0 + vs)
            turn_u = fv * (u0 + un)
            a = viscosity * u0
            c = viscosity * v0
            eu.append(a - p0 + turn_v)
            wu.append(a)
            ru.append(viscosity * (un + us) - 4.0 * a + p0 + turn_v)
            ev.append(c)
            wv.append(c - turn_u)
            rv.append(viscosity * (vn + vs) - 4.0 * c + (p0 - pn) - turn_u)
            u0s.append(u0)
            v0s.append(v0)
        eu, wu, ev, wv = eastward(*eu), westward(*wu), eastward(*ev), westward(*wv)
        for t in range(2):
            tend_u = jnp.where((lo_u[t] <= k) & (up_u[t] > k), eu[t] + wu[t] + ru[t], 0.0)
            tend_v = jnp.where((lo_v[t] <= k) & (up_v[t] > k), ev[t] + wv[t] + rv[t], 0.0)
            force_u[t] = force_u[t] + tend_u
            force_v[t] = force_v[t] + tend_v
            new_u = u0s[t] + step_time * tend_u
            new_v = v0s[t] + step_time * tend_v
            new_u = jnp.where(up_u[t] == k + 1, drag * new_u, new_u)
            new_v = jnp.where(up_v[t] == k + 1, drag * new_v, new_v)
            total_u[t] = total_u[t] + new_u
            total_v[t] = total_v[t] + new_v
            u_new[k, t, rows, :] = new_u
            v_new[k, t, rows, :] = new_v
    for t in range(2):
        flat[G_U, t, rows, :] = (substep_time * layer) * force_u[t]
        flat[G_V, t, rows, :] = (substep_time * layer) * force_v[t]
        flat[NEW_U, t, rows, :] = layer * total_u[t]
        flat[NEW_V, t, rows, :] = layer * total_v[t]


def inner_rows(own_ref, ea_ref, eb_ref, ft_ref, fv_ref, u_all, v_all, p_all, u_new, v_new, sums, bed, start, flow_u, flow_v, height, flat):
    even_lon = lax.rem(lax.axis_index("lon"), 2) == 0
    place = [u_all.at[k] for k in range(LEVELS)] + [v_all.at[k] for k in range(LEVELS)]
    place += [p_all.at[k] for k in range(LEVELS)] + [flat.at[BED], flat.at[FROM], height]
    for pack in range(PACKS):
        for at in range(0, ROWS, 32):
            a, b = ea_ref[pack, pl.ds(at, 32), :], eb_ref[pack, pl.ds(at, 32), :]
            east, west = jnp.where(even_lon, a, b), jnp.where(even_lon, b, a)
            tiles = [beside(east, west, p) for p in planes_of(pack)]
            for p, tile in zip(planes_of(pack), tiles):
                place[p][0, pl.ds(PAD + OWN + at, 32), :] = own_ref[p, pl.ds(at, 32), :]
                place[p][1, pl.ds(PAD + OWN + at, 32), :] = tile
    faces(OWN, 48, flat, ft_ref, fv_ref, False)
    faces(OWN + 48, 40, flat, ft_ref, fv_ref, False)

    def first(r, carry):
        mask_rows(r, flat, u_all, v_all, flow_u, flow_v)
        return carry

    def second(r, carry):
        tendencies(r, flat, ft_ref, fv_ref, u_all, v_all, p_all, u_new, v_new)
        return carry

    lax.fori_loop(INNER[0] - 1, INNER[1] + 1, first, 0)
    lax.fori_loop(INNER[0], INNER[1], second, 0)
    own = pl.ds(PAD + OWN, ROWS)
    inner = pl.ds(PAD + 8 * INNER[0], 8 * (INNER[1] - INNER[0]))
    for t in range(2):
        bed[t, own, :] = flat[BED, t, own, :]
        start[t, own, :] = flat[FROM, t, own, :]
        for i, which in enumerate(SUMS):
            sums[i, t, inner, :] = flat[which, t, inner, :]


def ocean_steps(
    na_ref, nb_ref, ft_ref, fv_ref, u_in, v_in, p_in, u_done, v_done, sums, bed, start, flow_u_in, flow_v_in, height_in,
    u_out, v_out, h_out,
    u_all, v_all, p_all, u_new, v_new,
    flat, flow_u, flow_v, height,
):
    lat = lax.axis_index("lat")
    even_lat = lax.rem(lat, 2) == 0
    even_lon = lax.rem(lax.axis_index("lon"), 2) == 0
    top = lat == lax.axis_size("lat") - 1
    place = [u_all.at[k] for k in range(LEVELS)] + [v_all.at[k] for k in range(LEVELS)]
    place += [p_all.at[k] for k in range(LEVELS)] + [flat.at[BED], flat.at[FROM], height]

    def north_rows(p):
        return jnp.where(even_lat, na_ref[pl.ds(p * HALO, HALO), :], nb_ref[pl.ds(p * FOLD, HALO), :])

    def south_rows(p):
        return jnp.where(even_lat, nb_ref[pl.ds(p * FOLD + FOLD - HALO, HALO), :], na_ref[pl.ds(p * HALO, HALO), :])

    own = pl.ds(PAD + OWN, ROWS)
    low = pl.ds(PAD + OWN, 8 * (INNER[0] + 1) - OWN)
    high = pl.ds(PAD + 8 * (INNER[1] - 1), OWN + ROWS - 8 * (INNER[1] - 1))
    inner = pl.ds(PAD + 8 * INNER[0], 8 * (INNER[1] - INNER[0]))
    masked = pl.ds(PAD + 8 * (INNER[0] - 1), 8 * (INNER[1] - INNER[0] + 2))
    for t in range(2):
        for k in range(LEVELS):
            p_all[k, t, own, :] = p_in[k, t, own, :]
            for rows in (low, high):
                u_all[k, t, rows, :] = u_in[k, t, rows, :]
                v_all[k, t, rows, :] = v_in[k, t, rows, :]
        flat[BED, t, own, :] = bed[t, own, :]
        flat[FROM, t, own, :] = start[t, own, :]
        height[t, own, :] = height_in[t, own, :]
        flow_u[0, t, masked, :] = flow_u_in[0, t, masked, :]
        flow_v[0, t, masked, :] = flow_v_in[0, t, masked, :]
        for i, which in enumerate(SUMS):
            flat[which, t, inner, :] = sums[i, t, inner, :]
            flat[which, t, pl.ds(PAD + EXT - 8, 8), :] = jnp.zeros((8, LANES), jnp.float32)

    edge, after = pl.ds(0, PAD), pl.ds(PAD + OWN + ROWS + HALO, 16)
    for pack in range(PACKS):
        pa, pb = PLANES + pack, PLANES + PACKS + pack
        for rows, at in ((south_rows, PAD), (north_rows, PAD + OWN + ROWS)):
            a, b = rows(pa), rows(pb)
            east, west = jnp.where(even_lon, a, b), jnp.where(even_lon, b, a)
            tiles = [(rows(p), beside(east, west, p)) for p in planes_of(pack)]
            for p, (t0, t1) in zip(planes_of(pack), tiles):
                place[p][0, pl.ds(at, HALO), :] = t0
                place[p][1, pl.ds(at, HALO), :] = t1
        for p in planes_of(pack):
            for t in range(2):
                place[p][t, edge, :] = jnp.full((PAD, LANES), beyond(p), jnp.float32)
                place[p][t, after, :] = jnp.full((16, LANES), beyond(p), jnp.float32)

    @pl.when(top)
    def _():
        lane = lanes_of((24, LANES))

        def flipped(x):
            return jnp.take_along_axis(x, LANES - 1 - lane, axis=1)

        for pack in range(PACKS):
            a = flipped(nb_ref[pl.ds((PLANES + pack) * FOLD, 24), :])
            b = flipped(nb_ref[pl.ds((PLANES + PACKS + pack) * FOLD, 24), :])
            east, west = jnp.where(even_lon, b, a), jnp.where(even_lon, a, b)
            tiles = []
            for p in planes_of(pack):
                slot = HALO * (p % 8)
                e = pltpu.roll(west, (slot + HALO) % LANES, 1) if slot != LANES - HALO else west
                w = pltpu.roll(east, slot, 1) if slot else east
                t0 = flipped(nb_ref[pl.ds(p * FOLD, 24), :])
                t1 = jnp.where(lane < HALO, e, jnp.where(lane >= LANES - HALO, w, beyond(p)))
                if p < LEVELS:
                    t0, t1 = eastward(t0, t1)
                    t0, t1 = -t0, -t1
                tiles.append((t0, t1))
            for p, (t0, t1) in zip(planes_of(pack), tiles):
                place[p][0, pl.ds(PAD + PATCH, FOLD), :] = t0[:FOLD]
                place[p][1, pl.ds(PAD + PATCH, FOLD), :] = t1[:FOLD]

    fold_ghosts(flat.at[BED], top)
    for at, n in CHUNKS:
        faces(at, n, flat, ft_ref, fv_ref, top)
    for flow in (flow_u, flow_v):
        for now in range(2):
            for t in range(2):
                flow[now, t, edge, :] = jnp.zeros((PAD, LANES), jnp.float32)
                flow[now, t, pl.ds(PAD + EXT, PAD), :] = jnp.zeros((PAD, LANES), jnp.float32)

    def mask_first(r, carry):
        mask_rows(r, flat, u_all, v_all, flow_u, flow_v)
        return carry

    lax.fori_loop(0, INNER[0] - 1, mask_first, 0)
    lax.fori_loop(INNER[1] + 1, EXT // 8, mask_first, 0)

    for step in range(STEPS):
        last = step == STEPS - 1
        for k in range(LEVELS):
            fold_ghosts(u_all.at[k], top)
            fold_ghosts(v_all.at[k], top, -1.0)
            if step == 0:
                fold_ghosts(p_all.at[k], top)
        fold_ghosts(flow_u.at[0], top)

        def tend(r, carry):
            tendencies(r, flat, ft_ref, fv_ref, u_all, v_all, p_all, u_new, v_new)
            return carry

        if last:
            lax.fori_loop(1, jnp.where(top, EXT // 8, EXT // 8 - 2), tend, 0)
        else:
            lax.fori_loop(0, INNER[0], tend, 0)
            lax.fori_loop(INNER[1], jnp.where(top, EXT // 8, EXT // 8 - 1), tend, 0)
        for which in (SUM_U, SUM_V):
            for t in range(2):
                flat[which, t, pl.ds(PAD, EXT), :] = jnp.zeros((EXT, LANES), jnp.float32)

        def substep(now, later):
            for at, n in CHUNKS:
                rows, down = pl.ds(PAD + at, n), pl.ds(PAD + at - 1, n)
                u = [flow_u[now, t, rows, :] for t in range(2)]
                uw = westward(*u)
                for t in range(2):
                    spread = u[t] - uw[t] + flow_v[now, t, rows, :] - flow_v[now, t, down, :]
                    height[t, rows, :] = height[t, rows, :] - flat[SEA, t, rows, :] * spread
            fold_ghosts(height, top)
            for at, n in CHUNKS:
                rows, up, down = pl.ds(PAD + at, n), pl.ds(PAD + at + 1, n), pl.ds(PAD + at - 1, n)
                h = [height[t, rows, :] for t in range(2)]
                he = eastward(*h)
                qv = [flow_v[now, t, rows, :] + flow_v[now, t, down, :] for t in range(2)]
                qve = eastward(*qv)
                qu = [flow_u[now, t, rows, :] + flow_u[now, t, up, :] for t in range(2)]
                quw = westward(*qu)
                for t in range(2):
                    next_u = (
                        flow_u[now, t, rows, :]
                        + flat[C_U, t, rows, :] * (he[t] - h[t])
                        + flat[F_U, t, rows, :] * (qv[t] + qve[t])
                        + flat[G_U, t, rows, :]
                    )
                    next_v = (
                        flow_v[now, t, rows, :]
                        + flat[C_V, t, rows, :] * (height[t, up, :] - h[t])
                        + flat[F_V, t, rows, :] * (qu[t] + quw[t])
                        + flat[G_V, t, rows, :]
                    )
                    flow_u[later, t, rows, :] = next_u
                    flow_v[later, t, rows, :] = next_v
                    flat[SUM_U, t, rows, :] = flat[SUM_U, t, rows, :] + next_u
                    flat[SUM_V, t, rows, :] = flat[SUM_V, t, rows, :] + next_v
            fold_ghosts(flow_u.at[later], top)

        def two_substeps(turn, carry):
            substep(0, 1)
            substep(1, 0)
            return carry

        lax.fori_loop(0, SUBSTEPS // 2, two_substeps, 0)

        def correct(r, u_from, v_from):
            rows = pl.ds(pl.multiple_of(r * 8, 8) + PAD, 8)
            for t in range(1 if last else 2):
                lo_u, up_u = flat[LO_U, t, rows, :], flat[UP_U, t, rows, :]
                lo_v, up_v = flat[FROM, t, rows, :], flat[UP_V, t, rows, :]
                mean_u = flat[SUM_U, t, rows, :] / SUBSTEPS
                mean_v = flat[SUM_V, t, rows, :] / SUBSTEPS
                depth_u = layer * jnp.maximum(up_u - lo_u, 1.0)
                depth_v = layer * jnp.maximum(up_v - lo_v, 1.0)
                add_u = (mean_u - flat[NEW_U, t, rows, :]) / depth_u
                add_v = (mean_v - flat[NEW_V, t, rows, :]) / depth_v
                us = [jnp.where((lo_u <= k) & (up_u > k), u_from[k, t, rows, :] + add_u, 0.0) for k in range(LEVELS)]
                vs = [jnp.where((lo_v <= k) & (up_v > k), v_from[k, t, rows, :] + add_v, 0.0) for k in range(LEVELS)]
                for k in range(LEVELS):
                    if last:
                        out = pl.ds(pl.multiple_of(r * 8 - OWN, 8), 8)
                        u_out[k, out, :] = us[k]
                        v_out[k, out, :] = vs[k]
                    else:
                        u_all[k, t, rows, :] = us[k]
                        v_all[k, t, rows, :] = vs[k]
                if not last:
                    flow_u[0, t, rows, :] = mean_u
                    flow_v[0, t, rows, :] = mean_v

        def correct_here(r, carry):
            correct(r, u_new, v_new)
            return carry

        def correct_inner(r, carry):
            correct(r, u_done, v_done)
            return carry

        if last:
            lax.fori_loop(OWN // 8, (OWN + ROWS) // 8, correct_here, 0)
        else:
            lax.fori_loop(0, INNER[0], correct_here, 0)
            lax.fori_loop(INNER[0], INNER[1], correct_inner, 0)
            lax.fori_loop(INNER[1], EXT // 8, correct_here, 0)

    h_out[...] = height[0, pl.ds(PAD + OWN, ROWS), :]


def lon_swaps():
    count = lax.axis_size("lon")
    first = [(i, i ^ 1) for i in range(count)]
    second = [(i, (((i + 1) % count) ^ 1) - 1) for i in range(count)]
    return first, [(i, j % count) for i, j in second]


def lat_swaps():
    lats, lons = lax.axis_size("lat"), lax.axis_size("lon")
    first, second = [], []
    for lat in range(lats):
        for lon in range(lons):
            first.append((lon * lats + lat, lon * lats + (lat ^ 1)))
            if lat == lats - 1:
                second.append((lon * lats + lat, (lons - 1 - lon) * lats + lat))
            elif lat:
                second.append((lon * lats + lat, lon * lats + ((lat + 1) ^ 1) - 1))
    return first, second


def turning(lat):
    lats = lax.axis_size("lat")
    ext = jnp.arange(TALL, dtype=jnp.int32) - PAD
    mirror = (lat == lats - 1) & (ext >= PATCH)
    row = jnp.where(mirror, lats * ROWS - FOLD + ext - PATCH, lat * ROWS + ext - OWN).astype(jnp.float32)
    sign = jnp.where(mirror, -0.25 * coriolis, 0.25 * coriolis)
    cells = lats * ROWS
    centre = sign * jnp.sin(math.pi * ((row + 0.5) / cells - 0.5))
    face = sign * jnp.sin(math.pi * ((row + 1.0) / cells - 0.5))
    wide = (TALL, LANES)
    return jnp.broadcast_to(centre[:, None], wide), jnp.broadcast_to(face[:, None], wide)


def whole(*shape):
    return pl.BlockSpec(shape, lambda *_: (0,) * len(shape))


def shards(u_velocity, v_velocity, density, surface, land_mask, bottom):
    f32 = jnp.float32
    params = pltpu.CompilerParams(vmem_limit_bytes=VMEM_LIMIT)
    level_block = (LEVELS, ROWS, LANES)
    fields = (u_velocity, v_velocity, density, surface, land_mask, bottom)
    pack_a, pack_b = pl.pallas_call(
        strips,
        out_shape=(jax.ShapeDtypeStruct((PACKS, ROWS, LANES), f32),) * 2,
        in_specs=[pl.BlockSpec(memory_space=pltpu.HBM)] * 6,
        scratch_shapes=[pltpu.VMEM(level_block, f32)] * 3
        + [pltpu.VMEM((ROWS, LANES), f32), pltpu.VMEM(level_block, jnp.int32), pltpu.VMEM((ROWS, LANES), jnp.int32)]
        + [pltpu.SemaphoreType.DMA((6,))],
        compiler_params=pltpu.CompilerParams(vmem_limit_bytes=56 * 1024 * 1024),
    )(*fields)
    lon_first, lon_second = lon_swaps()
    east_a = lax.ppermute(pack_a, "lon", lon_first)
    east_b = lax.ppermute(pack_b, "lon", lon_second)
    own = pl.pallas_call(
        own_block,
        out_shape=jax.ShapeDtypeStruct((PLANES, ROWS, LANES), f32),
        compiler_params=pltpu.CompilerParams(vmem_limit_bytes=8 * 1024 * 1024),
        cost_estimate=pl.CostEstimate(flops=4000000, bytes_accessed=5000000, transcendentals=0),
    )(*fields)

    low = lambda planes: pl.BlockSpec((planes, 24, LANES), lambda i: (0, 0, 0))
    high = lambda planes: pl.BlockSpec((planes, 24, LANES), lambda i: (0, ROWS // 24 - 1, 0))
    rows_a, rows_b = pl.pallas_call(
        outer_rows,
        grid=(1,),
        in_specs=[low(PLANES), low(PACKS), low(PACKS), high(PLANES), high(PACKS), high(PACKS)],
        out_specs=(whole(SENT * HALO, LANES), whole(888, LANES)),
        out_shape=(
            jax.ShapeDtypeStruct((SENT * HALO, LANES), f32),
            jax.ShapeDtypeStruct((888, LANES), f32),
        ),
        compiler_params=params,
    )(own, east_a, east_b, own, east_a, east_b)
    lat_first, lat_second = lat_swaps()
    north_b = lax.ppermute(rows_b, ("lon", "lat"), lat_second)
    north_a = lax.ppermute(rows_a, ("lon", "lat"), lat_first)

    turn_centre, turn_face = turning(lax.axis_index("lat"))
    levels, pair, single = (LEVELS, 2, TALL, LANES), (2, 2, TALL, LANES), (2, TALL, LANES)
    shapes = [levels] * 5 + [(len(SUMS), 2, TALL, LANES), single, single, (1, 2, TALL, LANES), (1, 2, TALL, LANES), single]
    done = pl.pallas_call(
        inner_rows,
        out_shape=tuple(jax.ShapeDtypeStruct(shape, f32) for shape in shapes),
        scratch_shapes=[pltpu.VMEM((16, 2, TALL, LANES), f32)],
        compiler_params=params,
        cost_estimate=pl.CostEstimate(flops=40000000, bytes_accessed=12000000, transcendentals=0),
    )(own, east_a, east_b, turn_centre, turn_face)
    return pl.pallas_call(
        ocean_steps,
        out_shape=(
            jax.ShapeDtypeStruct(level_block, f32),
            jax.ShapeDtypeStruct(level_block, f32),
            jax.ShapeDtypeStruct((ROWS, LANES), f32),
        ),
        scratch_shapes=[pltpu.VMEM(levels, f32)] * 5
        + [pltpu.VMEM((16, 2, TALL, LANES), f32)]
        + [pltpu.VMEM(pair, f32), pltpu.VMEM(pair, f32), pltpu.VMEM(single, f32)],
        compiler_params=params,
    )(north_a, north_b, turn_centre, turn_face, *done)


def solution(mesh):
    return jax.shard_map(
        shards,
        mesh=mesh,
        in_specs=(
            P(None, "lat", "lon"),
            P(None, "lat", "lon"),
            P(None, "lat", "lon"),
            P("lat", "lon"),
            P(None, "lat", "lon"),
            P("lat", "lon"),
        ),
        out_specs=(P(None, "lat", "lon"), P(None, "lat", "lon"), P("lat", "lon")),
        check_vma=False,
    )
```

time: 61.4 us -> 50.9 us (0.83); the launches traced: 60.6 us -> 50.8 us
  waiting for transfers between devices: 21.5 us -> 17.4 us
  Pallas kernels: 23.4 us -> 19.6 us
  local copies, waits for them, and re-layouts: 2.24 us -> 0.18 us
    pallas_call x1, Pallas kernels: 17.3 us -> 11.3 us  [shards(): pl.pallas_call(ocean_steps, out_shape=(jax.ShapeDtypeStruct(level_block,...]
    pallas_call x1 -> x3, Pallas kernels: 3.91 us -> 7.3 us  [the longest x1 3.48 us: shards(): pl.pallas_call(inner_rows, out_shape=tuple((jax.ShapeDtypeStruct(shape, f...]
    ppermute x1, waiting for transfers between devices: 1.86 us -> 0.01 us  [shards(): north_a = lax.ppermute(rows_a, ('lon', 'lat'), lat_first)]
    ppermute x1, waiting for transfers between devices: 14 us -> 12.2 us  [shards(): north_b = lax.ppermute(rows_b, ('lon', 'lat'), lat_second)]
    pallas_call x1, Pallas kernels: 2.2 us -> 0.98 us  [shards(): pl.pallas_call(outer_rows, grid=(1,), in_specs=[low(PLANES), low(PACKS),...]
    broadcast_in_dim x1, local copies, waits for them, and re-layouts: 0.82 us -> 0.08 us  [turning(): jnp.broadcast_to(face[:, None], wide)]
    unnamed x8 -> x12, local copies, waits for them, and re-layouts: 0.7 us -> 0.03 us
    broadcast_in_dim x1, local copies, waits for them, and re-layouts: 0.73 us -> 0.08 us  [turning(): jnp.broadcast_to(centre[:, None], wide)]
  transfers between devices with their start and end apart: 4 -> 4, of which waited for: 3 -> 2; matrix products, arithmetic and copies ran while one was open for 0% -> 0% of each run, Pallas kernels for 0% -> 8%
where the time goes in v2:
time: 50.9 us; the launch traced here: 50.8 us
  Pallas kernels  19.6 us (39%)
  waiting for transfers between devices  17.4 us (34%)
  starting transfers between devices  12.8 us (25%)
  between operations  0.78 us (2%)
    ppermute x1, waiting for transfers between devices, shards(): north_b = lax.ppermute(rows_b, ('lon', 'lat'), lat_second)  12.2 us
    pallas_call x1, Pallas kernels, shards(): pl.pallas_call(ocean_steps, out_shape=(jax.ShapeDtypeStruct(level_block,...  11.3 us
    ppermute x1, starting transfers between devices, shards(): east_b = lax.ppermute(pack_b, 'lon', lon_second)  7.3 us
    ppermute x1, waiting for transfers between devices, shards(): east_b = lax.ppermute(pack_b, 'lon', lon_second)  5.13 us
    ppermute x1, starting transfers between devices, shards(): north_b = lax.ppermute(rows_b, ('lon', 'lat'), lat_second)  3.73 us
    pallas_call x1, Pallas kernels, shards(): pl.pallas_call(inner_rows, out_shape=tuple((jax.ShapeDtypeStruct(shape, f...  3.48 us
    pallas_call x1, Pallas kernels, shards(): pl.pallas_call(strips, out_shape=(jax.ShapeDtypeStruct((PACKS, ROWS, LANE...  3.42 us
    ppermute x1, starting transfers between devices, shards(): east_a = lax.ppermute(pack_a, 'lon', lon_first)  1.72 us
  transfers between devices with their start and end apart: 4, of which 2 were waited for; matrix products, arithmetic and copies ran while one was open for 0% of the time, Pallas kernels for 8%

profile of v2, /device:TPU:7, one launch (start us, length us, event | category | flops | bytes accessed | tf_op | source)
XLA Modules:
  0.0 50.8 jit_solution(9434867068023838323)
XLA Ops:
  0.6 0.0 copy-start.3
  0.6 0.0 copy-start.5
  0.7 0.0 copy-start
  0.7 0.0 copy-start.1
  0.7 0.0 copy-start.2
  0.7 0.0 copy-start.4
  0.7 3.4 %shard_map.86 = (f32[5,96,128]{2,1,0:T(8,128)}, f32[5,96,128]{2,1,0:T(8,128)}) custom-call(f32[12,96,128]{2,1,0:T(8,128)} %u_far.1, f32[12,96,128]{2,1,0:T(8,128)} %v_far.1, f32[12,96,128]{2,1,0:T(8,128)} %d_far.1, f32[96,128]{1,0:T(8,128)} %s_far.1, s32[12,96,128]{2,1,0:T(8,128)} %m_far.1, s32[96,128]{1,0:T(8,128)} %b_far.1), custom_call_target="tpu_custom_call" | custom-call | tf_op jit(solution)/shard_map/pallas_call | solution.py:520
  4.1 1.7 %collective-permute-start = (f32[5,96,128]{2,1,0:T(8,128)}, f32[5,96,128]{2,1,0:T(8,128)S(1)}, u32[]{:S(2)}, u32[]{:S(2)}) collective-permute-start(f32[5,96,128]{2,1,0:T(8,128)} %get-tuple-element.18), channel_id=1, source_target_pairs={{0,16},{16,0},{32,48},{48,32},{64,80},{80,64},{96,112},{112,96},{1... | collective-permute-start | bytes 737288 | tf_op jit(solution)/shard_map/ppermute | solution.py:530
  5.8 7.3 %collective-permute-start.1 = (f32[5,96,128]{2,1,0:T(8,128)}, f32[5,96,128]{2,1,0:T(8,128)S(1)}, u32[]{:S(2)}, u32[]{:S(2)}) collective-permute-start(f32[5,96,128]{2,1,0:T(8,128)} %get-tuple-element.19), channel_id=1, source_target_pairs={{0,240},{16,32},{32,16},{48,64},{64,48},{80,96},{96,80},{112,128},... | collective-permute-start | bytes 737288 | tf_op jit(solution)/shard_map/ppermute | solution.py:531
  13.1 0.0 copy-done.5
  13.2 0.0 copy-done.1
  13.2 0.4 shard_map.85.low_own.top_own.own_ref
  13.6 0.0 collective-permute-done.low_a.top_a.ea_ref
  13.6 5.1 %collective-permute-done.1.low_b.top_b.eb_ref = f32[5,96,128]{2,1,0:T(8,128)S(1)} collective-permute-done((f32[5,96,128]{2,1,0:T(8,128)}, f32[5,96,128]{2,1,0:T(8,128)S(1)}, u32[]{:S(2)}, u32[]{:S(2)}) %collective-permute-start.1) | collective-permute-done | bytes 245792 | tf_op jit(solution)/shard_map/ppermute | solution.py:531
  18.7 1.0 %shard_map.87 = (f32[784,128]{1,0:T(8,128)}, f32[888,128]{1,0:T(8,128)}) custom-call(f32[39,96,128]{2,1,0:T(8,128)S(1)} %shard_map.85.low_own.top_own.own_ref, f32[5,96,128]{2,1,0:T(8,128)S(1)} %collective-permute-done.low_a.top_a.ea_ref, f32[5,96,128]{2,1,0:T(8,128)S(1)} %collective-permute-done.1.low_b.top_b.eb_ref, ...), custom_call_target="tpu_custom_call" | custom-call | tf_op jit(solution)/shard_map/pallas_call | solution.py:541
  19.7 3.7 %collective-permute-start.3 = (f32[888,128]{1,0:T(8,128)}, f32[888,128]{1,0:T(8,128)S(1)}, u32[]{:S(2)}, u32[]{:S(2)}) collective-permute-start(f32[888,128]{1,0:T(8,128)} %get-tuple-element.21), channel_id=1, source_target_pairs={{1,2},{17,18},{33,34},{49,50},{65,66},{81,82},{97,98},{113,114},{1... | collective-permute-start | bytes 1363976 | tf_op jit(solution)/shard_map/ppermute | solution.py:553
  23.4 0.1 collective-permute-start.2
  23.5 0.1 select_multiply_fusion
  23.6 0.1 broadcast_in_dim.22.ft_ref
  23.7 0.1 broadcast_in_dim.23.fv_ref
  23.8 3.5 %shard_map.88 = (f32[12,2,152,128]{3,2,1,0:T(8,128)S(1)}, f32[12,2,152,128]{3,2,1,0:T(8,128)S(1)}, f32[12,2,152,128]{3,2,1,0:T(8,128)S(1)}, f32[12,2,152,128]{3,...) custom-call(f32[39,96,128]{2,1,0:T(8,128)S(1)} %shard_map.85.low_own, ...), custom_call_target="tpu_custom_call" | custom-call | flops 40000000 | bytes 12000000 | tf_op jit(solution)/shard_map/pallas_call | solution.py:559
  27.3 0.0 collective-permute-done.2.na_ref
  27.3 12.2 %collective-permute-done.3.nb_ref = f32[888,128]{1,0:T(8,128)S(1)} collective-permute-done((f32[888,128]{1,0:T(8,128)}, f32[888,128]{1,0:T(8,128)S(1)}, u32[]{:S(2)}, u32[]{:S(2)}) %collective-permute-start.3) | collective-permute-done | bytes 454688 | tf_op jit(solution)/shard_map/ppermute | solution.py:553
  39.5 11.3 %shard_map.89 = (f32[12,96,128]{2,1,0:T(8,128)}, f32[12,96,128]{2,1,0:T(8,128)}, f32[96,128]{1,0:T(8,128)}) custom-call(f32[784,128]{1,0:T(8,128)S(1)} %collective-permute-done.2.na_ref, f32[888,128]{1,0:T(8,128)S(1)} %collective-permute-done.3.nb_ref, f32[152,128]{1,0:T(8,128)S(1)} %broadcast_in_dim.22.ft_ref, f32[152,128]{1,0:T(8,128)S(1)} %broadcast_in_dim.23.fv_ref, ...), custom_call_target="tpu_custom_call" | custom-call | tf_op jit(solution)/shard_map/pallas_call | solution.py:566
  (4 shorter events, 0.0 us)
Async XLA Ops:
  0.6 12.5 %copy-start.3 = (s32[12,96,128]{2,1,0:T(8,128)S(1)}, s32[12,96,128]{2,1,0:T(8,128)}, u32[]{:S(2)}) copy-start(s32[12,96,128]{2,1,0:T(8,128)} %m_far.1) | copy-start | bytes 1769476
  0.6 12.5 %copy-start.5 = (s32[96,128]{1,0:T(8,128)S(1)}, s32[96,128]{1,0:T(8,128)}, u32[]{:S(2)}) copy-start(s32[96,128]{1,0:T(8,128)} %b_far.1) | copy-start | bytes 147460
  0.7 12.5 %copy-start = (f32[12,96,128]{2,1,0:T(8,128)S(1)}, f32[12,96,128]{2,1,0:T(8,128)}, u32[]{:S(2)}) copy-start(f32[12,96,128]{2,1,0:T(8,128)} %u_far.1) | copy-start | bytes 1769476
  0.7 12.5 %copy-start.1 = (f32[12,96,128]{2,1,0:T(8,128)S(1)}, f32[12,96,128]{2,1,0:T(8,128)}, u32[]{:S(2)}) copy-start(f32[12,96,128]{2,1,0:T(8,128)} %v_far.1) | copy-start | bytes 1769476
  0.7 12.5 %copy-start.2 = (f32[12,96,128]{2,1,0:T(8,128)S(1)}, f32[12,96,128]{2,1,0:T(8,128)}, u32[]{:S(2)}) copy-start(f32[12,96,128]{2,1,0:T(8,128)} %d_far.1) | copy-start | bytes 1769476
  0.7 12.5 %copy-start.4 = (f32[96,128]{1,0:T(8,128)S(1)}, f32[96,128]{1,0:T(8,128)}, u32[]{:S(2)}) copy-start(f32[96,128]{1,0:T(8,128)} %s_far.1) | copy-start | bytes 147460
  4.1 9.5 %collective-permute-start = (f32[5,96,128]{2,1,0:T(8,128)}, f32[5,96,128]{2,1,0:T(8,128)S(1)}, u32[]{:S(2)}, u32[]{:S(2)}) collective-permute-start(f32[5,96,128]{2,1,0:T(8,128)} %get-tuple-element.18), channel_id=1, source_target_pairs={{0,16},{16,0},{32,48},{48,32},{64,80},{80,64},{96,112},{112,96},{1... | collective-permute-start | bytes 737288 | tf_op jit(solution)/shard_map/ppermute | solution.py:530
  5.8 12.9 %collective-permute-start.1 = (f32[5,96,128]{2,1,0:T(8,128)}, f32[5,96,128]{2,1,0:T(8,128)S(1)}, u32[]{:S(2)}, u32[]{:S(2)}) collective-permute-start(f32[5,96,128]{2,1,0:T(8,128)} %get-tuple-element.19), channel_id=1, source_target_pairs={{0,240},{16,32},{32,16},{48,64},{64,48},{80,96},{96,80},{112,128},... | collective-permute-start | bytes 737288 | tf_op jit(solution)/shard_map/ppermute | solution.py:531
  19.7 19.8 %collective-permute-start.3 = (f32[888,128]{1,0:T(8,128)}, f32[888,128]{1,0:T(8,128)S(1)}, u32[]{:S(2)}, u32[]{:S(2)}) collective-permute-start(f32[888,128]{1,0:T(8,128)} %get-tuple-element.21), channel_id=1, source_target_pairs={{1,2},{17,18},{33,34},{49,50},{65,66},{81,82},{97,98},{113,114},{1... | collective-permute-start | bytes 1363976 | tf_op jit(solution)/shard_map/ppermute | solution.py:553
  23.4 3.8 %collective-permute-start.2 = (f32[784,128]{1,0:T(8,128)}, f32[784,128]{1,0:T(8,128)S(1)}, u32[]{:S(2)}, u32[]{:S(2)}) collective-permute-start(f32[784,128]{1,0:T(8,128)} %get-tuple-element.20), channel_id=1, source_target_pairs={{0,1},{16,17},{32,33},{48,49},{64,65},{80,81},{96,97},{112,113},{1... | collective-permute-start | bytes 1204232 | tf_op jit(solution)/shard_map/ppermute | solution.py:554

commit v3 on v2

--- a/solution.py
+++ b/solution.py
@@ -131,6 +131,10 @@
 
 (BED, FROM, UP_U, LO_U, UP_V, C_U, F_U, G_U, C_V, F_V, G_V, SUM_U, SUM_V, NEW_U, NEW_V, SEA) = range(16)
 INNER = (3, 12)
+CORE = (4, 11)
+CORE_ROWS = (8 * CORE[0], 8 * (CORE[1] - CORE[0]))
+INNER_CHUNKS = ((24, 32), (56, 40))
+OUTER_CHUNKS = ((0, 40), (80, 24), (104, 32))
 SUMS = (G_U, G_V, NEW_U, NEW_V)
 
 
@@ -237,7 +241,95 @@
         flat[NEW_V, t, rows, :] = layer * total_v[t]
 
 
-def inner_rows(own_ref, ea_ref, eb_ref, ft_ref, fv_ref, u_all, v_all, p_all, u_new, v_new, sums, bed, start, flow_u, flow_v, height, flat):
+def substep(now, later, chunks, top, flat, flow_u, flow_v, height):
+    for at, n in chunks:
+        rows, down = pl.ds(PAD + at, n), pl.ds(PAD + at - 1, n)
+        u = [flow_u[now, t, rows, :] for t in range(2)]
+        uw = westward(*u)
+        for t in range(2):
+            spread = u[t] - uw[t] + flow_v[now, t, rows, :] - flow_v[now, t, down, :]
+            height[t, rows, :] = height[t, rows, :] - flat[SEA, t, rows, :] * spread
+    if top is not None:
+        fold_ghosts(height, top)
+    for at, n in chunks:
+        rows, up, down = pl.ds(PAD + at, n), pl.ds(PAD + at + 1, n), pl.ds(PAD + at - 1, n)
+        h = [height[t, rows, :] for t in range(2)]
+        he = eastward(*h)
+        qv = [flow_v[now, t, rows, :] + flow_v[now, t, down, :] for t in range(2)]
+        qve = eastward(*qv)
+        qu = [flow_u[now, t, rows, :] + flow_u[now, t, up, :] for t in range(2)]
+        quw = westward(*qu)
+        for t in range(2):
+            next_u = (
+                flow_u[now, t, rows, :]
+                + flat[C_U, t, rows, :] * (he[t] - h[t])
+                + flat[F_U, t, rows, :] * (qv[t] + qve[t])
+                + flat[G_U, t, rows, :]
+            )
+            next_v = (
+                flow_v[now, t, rows, :]
+                + flat[C_V, t, rows, :] * (height[t, up, :] - h[t])
+                + flat[F_V, t, rows, :] * (qu[t] + quw[t])
+                + flat[G_V, t, rows, :]
+            )
+            flow_u[later, t, rows, :] = next_u
+            flow_v[later, t, rows, :] = next_v
+            flat[SUM_U, t, rows, :] = flat[SUM_U, t, rows, :] + next_u
+            flat[SUM_V, t, rows, :] = flat[SUM_V, t, rows, :] + next_v
+    if top is not None:
+        fold_ghosts(flow_u.at[later], top)
+
+
+def substeps(chunks, top, flat, flow_u, flow_v, height):
+    for which in (SUM_U, SUM_V):
+        for t in range(2):
+            for at, n in chunks:
+                flat[which, t, pl.ds(PAD + at, n), :] = jnp.zeros((n, LANES), jnp.float32)
+
+    def two(turn, carry):
+        substep(0, 1, chunks, top, flat, flow_u, flow_v, height)
+        substep(1, 0, chunks, top, flat, flow_u, flow_v, height)
+        return carry
+
+    lax.fori_loop(0, SUBSTEPS // 2, two, 0)
+
+
+def correct(first, end, flat, u_from, v_from, u_to, v_to, flow_u, flow_v):
+    def tile(r, carry):
+        rows = pl.ds(pl.multiple_of(r * 8, 8) + PAD, 8)
+        last = flow_u is None
+        for t in range(1 if last else 2):
+            lo_u, up_u = flat[LO_U, t, rows, :], flat[UP_U, t, rows, :]
+            lo_v, up_v = flat[FROM, t, rows, :], flat[UP_V, t, rows, :]
+            mean_u = flat[SUM_U, t, rows, :] / SUBSTEPS
+            mean_v = flat[SUM_V, t, rows, :] / SUBSTEPS
+            depth_u = layer * jnp.maximum(up_u - lo_u, 1.0)
+            depth_v = layer * jnp.maximum(up_v - lo_v, 1.0)
+            add_u = (mean_u - flat[NEW_U, t, rows, :]) / depth_u
+            add_v = (mean_v - flat[NEW_V, t, rows, :]) / depth_v
+            us = [jnp.where((lo_u <= k) & (up_u > k), u_from[k, t, rows, :] + add_u, 0.0) for k in range(LEVELS)]
+            vs = [jnp.where((lo_v <= k) & (up_v > k), v_from[k, t, rows, :] + add_v, 0.0) for k in range(LEVELS)]
+            for k in range(LEVELS):
+                if last:
+                    out = pl.ds(pl.multiple_of(r * 8 - OWN, 8), 8)
+                    u_to[k, out, :] = us[k]
+                    v_to[k, out, :] = vs[k]
+                else:
+                    u_to[k, t, rows, :] = us[k]
+                    v_to[k, t, rows, :] = vs[k]
+            if not last:
+                flow_u[0, t, rows, :] = mean_u
+                flow_v[0, t, rows, :] = mean_v
+        return carry
+
+    lax.fori_loop(first, end, tile, 0)
+
+
+def inner_rows(
+    own_ref, ea_ref, eb_ref, ft_ref, fv_ref,
+    u_all, v_all, p_all, u_new, v_new, u_next, v_next, sums, later_sums, bed, start, flows, height_in, later,
+    flat, flow_u, flow_v, height,
+):
     even_lon = lax.rem(lax.axis_index("lon"), 2) == 0
     place = [u_all.at[k] for k in range(LEVELS)] + [v_all.at[k] for k in range(LEVELS)]
     place += [p_all.at[k] for k in range(LEVELS)] + [flat.at[BED], flat.at[FROM], height]
@@ -264,15 +356,38 @@
     lax.fori_loop(INNER[0], INNER[1], second, 0)
     own = pl.ds(PAD + OWN, ROWS)
     inner = pl.ds(PAD + 8 * INNER[0], 8 * (INNER[1] - INNER[0]))
+    masked = pl.ds(PAD + 8 * (INNER[0] - 1), 8 * (INNER[1] - INNER[0] + 2))
+    core = pl.ds(PAD + CORE_ROWS[0], CORE_ROWS[1])
     for t in range(2):
         bed[t, own, :] = flat[BED, t, own, :]
         start[t, own, :] = flat[FROM, t, own, :]
+        height_in[t, own, :] = height[t, own, :]
+        flows[0, t, masked, :] = flow_u[0, t, masked, :]
+        flows[1, t, masked, :] = flow_v[0, t, masked, :]
         for i, which in enumerate(SUMS):
             sums[i, t, inner, :] = flat[which, t, inner, :]
+        for flow in (flow_u, flow_v):
+            flow[1, t, pl.ds(PAD + 8 * INNER[0] - 8, 8), :] = jnp.zeros((8, LANES), jnp.float32)
+            flow[1, t, pl.ds(PAD + 8 * INNER[1], 8), :] = jnp.zeros((8, LANES), jnp.float32)
+    substeps(INNER_CHUNKS, None, flat, flow_u, flow_v, height)
+    correct(INNER[0], INNER[1], flat, u_new, v_new, u_next, v_next, flow_u, flow_v)
+
+    def third(r, carry):
+        tendencies(r, flat, ft_ref, fv_ref, u_next, v_next, p_all, u_new, v_new)
+        return carry
+
+    lax.fori_loop(CORE[0], CORE[1], third, 0)
+    for t in range(2):
+        later[0, t, core, :] = flow_u[0, t, core, :]
+        later[1, t, core, :] = flow_v[0, t, core, :]
+        later[2, t, core, :] = height[t, core, :]
+        for i, which in enumerate(SUMS):
+            later_sums[i, t, core, :] = flat[which, t, core, :]
 
 
 def ocean_steps(
-    na_ref, nb_ref, ft_ref, fv_ref, u_in, v_in, p_in, u_done, v_done, sums, bed, start, flow_u_in, flow_v_in, height_in,
+    na_ref, nb_ref, ft_ref, fv_ref,
+    u_in, v_in, p_in, u_done, v_done, u_next, v_next, sums, later_sums, bed, start, flows, height_in, later,
     u_out, v_out, h_out,
     u_all, v_all, p_all, u_new, v_new,
     flat, flow_u, flow_v, height,
@@ -291,21 +406,22 @@
         return jnp.where(even_lat, nb_ref[pl.ds(p * FOLD + FOLD - HALO, HALO), :], na_ref[pl.ds(p * HALO, HALO), :])
 
     own = pl.ds(PAD + OWN, ROWS)
-    low = pl.ds(PAD + OWN, 8 * (INNER[0] + 1) - OWN)
-    high = pl.ds(PAD + 8 * (INNER[1] - 1), OWN + ROWS - 8 * (INNER[1] - 1))
+    low = pl.ds(PAD + OWN, 8 * (CORE[0] + 1) - OWN)
+    high = pl.ds(PAD + 8 * (CORE[1] - 1), OWN + ROWS - 8 * (CORE[1] - 1))
+    core = pl.ds(PAD + CORE_ROWS[0], CORE_ROWS[1])
     inner = pl.ds(PAD + 8 * INNER[0], 8 * (INNER[1] - INNER[0]))
     masked = pl.ds(PAD + 8 * (INNER[0] - 1), 8 * (INNER[1] - INNER[0] + 2))
     for t in range(2):
         for k in range(LEVELS):
-            p_all[k, t, own, :] = p_in[k, t, own, :]
             for rows in (low, high):
+                p_all[k, t, rows, :] = p_in[k, t, rows, :]
                 u_all[k, t, rows, :] = u_in[k, t, rows, :]
                 v_all[k, t, rows, :] = v_in[k, t, rows, :]
         flat[BED, t, own, :] = bed[t, own, :]
         flat[FROM, t, own, :] = start[t, own, :]
         height[t, own, :] = height_in[t, own, :]
-        flow_u[0, t, masked, :] = flow_u_in[0, t, masked, :]
-        flow_v[0, t, masked, :] = flow_v_in[0, t, masked, :]
+        flow_u[0, t, masked, :] = flows[0, t, masked, :]
+        flow_v[0, t, masked, :] = flows[1, t, masked, :]
         for i, which in enumerate(SUMS):
             flat[which, t, inner, :] = sums[i, t, inner, :]
             flat[which, t, pl.ds(PAD + EXT - 8, 8), :] = jnp.zeros((8, LANES), jnp.float32)
@@ -367,111 +483,49 @@
     lax.fori_loop(0, INNER[0] - 1, mask_first, 0)
     lax.fori_loop(INNER[1] + 1, EXT // 8, mask_first, 0)
 
-    for step in range(STEPS):
-        last = step == STEPS - 1
+    def ghosts():
         for k in range(LEVELS):
             fold_ghosts(u_all.at[k], top)
             fold_ghosts(v_all.at[k], top, -1.0)
-            if step == 0:
-                fold_ghosts(p_all.at[k], top)
         fold_ghosts(flow_u.at[0], top)
 
-        def tend(r, carry):
-            tendencies(r, flat, ft_ref, fv_ref, u_all, v_all, p_all, u_new, v_new)
-            return carry
-
-        if last:
-            lax.fori_loop(1, jnp.where(top, EXT // 8, EXT // 8 - 2), tend, 0)
-        else:
-            lax.fori_loop(0, INNER[0], tend, 0)
-            lax.fori_loop(INNER[1], jnp.where(top, EXT // 8, EXT // 8 - 1), tend, 0)
-        for which in (SUM_U, SUM_V):
-            for t in range(2):
-                flat[which, t, pl.ds(PAD, EXT), :] = jnp.zeros((EXT, LANES), jnp.float32)
-
-        def substep(now, later):
-            for at, n in CHUNKS:
-                rows, down = pl.ds(PAD + at, n), pl.ds(PAD + at - 1, n)
-                u = [flow_u[now, t, rows, :] for t in range(2)]
-                uw = westward(*u)
-                for t in range(2):
-                    spread = u[t] - uw[t] + flow_v[now, t, rows, :] - flow_v[now, t, down, :]
-                    height[t, rows, :] = height[t, rows, :] - flat[SEA, t, rows, :] * spread
-            fold_ghosts(height, top)
-            for at, n in CHUNKS:
-                rows, up, down = pl.ds(PAD + at, n), pl.ds(PAD + at + 1, n), pl.ds(PAD + at - 1, n)
-                h = [height[t, rows, :] for t in range(2)]
-                he = eastward(*h)
-                qv = [flow_v[now, t, rows, :] + flow_v[now, t, down, :] for t in range(2)]
-                qve = eastward(*qv)
-                qu = [flow_u[now, t, rows, :] + flow_u[now, t, up, :] for t in range(2)]
-                quw = westward(*qu)
-                for t in range(2):
-                    next_u = (
-                        flow_u[now, t, rows, :]
-                        + flat[C_U, t, rows, :] * (he[t] - h[t])
-                        + flat[F_U, t, rows, :] * (qv[t] + qve[t])
-                        + flat[G_U, t, rows, :]
-                    )
-                    next_v = (
-                        flow_v[now, t, rows, :]
-                        + flat[C_V, t, rows, :] * (height[t, up, :] - h[t])
-                        + flat[F_V, t, rows, :] * (qu[t] + quw[t])
-                        + flat[G_V, t, rows, :]
-                    )
-                    flow_u[later, t, rows, :] = next_u
-                    flow_v[later, t, rows, :] = next_v
-                    flat[SUM_U, t, rows, :] = flat[SUM_U, t, rows, :] + next_u
-                    flat[SUM_V, t, rows, :] = flat[SUM_V, t, rows, :] + next_v
-            fold_ghosts(flow_u.at[later], top)
-
-        def two_substeps(turn, carry):
-            substep(0, 1)
-            substep(1, 0)
-            return carry
-
-        lax.fori_loop(0, SUBSTEPS // 2, two_substeps, 0)
-
-        def correct(r, u_from, v_from):
-            rows = pl.ds(pl.multiple_of(r * 8, 8) + PAD, 8)
-            for t in range(1 if last else 2):
-                lo_u, up_u = flat[LO_U, t, rows, :], flat[UP_U, t, rows, :]
-                lo_v, up_v = flat[FROM, t, rows, :], flat[UP_V, t, rows, :]
-                mean_u = flat[SUM_U, t, rows, :] / SUBSTEPS
-                mean_v = flat[SUM_V, t, rows, :] / SUBSTEPS
-                depth_u = layer * jnp.maximum(up_u - lo_u, 1.0)
-                depth_v = layer * jnp.maximum(up_v - lo_v, 1.0)
-                add_u = (mean_u - flat[NEW_U, t, rows, :]) / depth_u
-                add_v = (mean_v - flat[NEW_V, t, rows, :]) / depth_v
-                us = [jnp.where((lo_u <= k) & (up_u > k), u_from[k, t, rows, :] + add_u, 0.0) for k in range(LEVELS)]
-                vs = [jnp.where((lo_v <= k) & (up_v > k), v_from[k, t, rows, :] + add_v, 0.0) for k in range(LEVELS)]
-                for k in range(LEVELS):
-                    if last:
-                        out = pl.ds(pl.multiple_of(r * 8 - OWN, 8), 8)
-                        u_out[k, out, :] = us[k]
-                        v_out[k, out, :] = vs[k]
-                    else:
-                        u_all[k, t, rows, :] = us[k]
-                        v_all[k, t, rows, :] = vs[k]
-                if not last:
-                    flow_u[0, t, rows, :] = mean_u
-                    flow_v[0, t, rows, :] = mean_v
-
-        def correct_here(r, carry):
-            correct(r, u_new, v_new)
-            return carry
-
-        def correct_inner(r, carry):
-            correct(r, u_done, v_done)
-            return carry
-
-        if last:
-            lax.fori_loop(OWN // 8, (OWN + ROWS) // 8, correct_here, 0)
-        else:
-            lax.fori_loop(0, INNER[0], correct_here, 0)
-            lax.fori_loop(INNER[0], INNER[1], correct_inner, 0)
-            lax.fori_loop(INNER[1], EXT // 8, correct_here, 0)
-
+    def tend(r, carry):
+        tendencies(r, flat, ft_ref, fv_ref, u_all, v_all, p_all, u_new, v_new)
+        return carry
+
+    for k in range(LEVELS):
+        fold_ghosts(p_all.at[k], top)
+    ghosts()
+    lax.fori_loop(0, INNER[0], tend, 0)
+    lax.fori_loop(INNER[1], jnp.where(top, EXT // 8, EXT // 8 - 1), tend, 0)
+    for flow in (flow_u, flow_v):
+        for t in range(2):
+            for at in (40, 72):
+                flow[1, t, pl.ds(PAD + at, 8), :] = jnp.zeros((8, LANES), jnp.float32)
+    substeps(OUTER_CHUNKS, top, flat, flow_u, flow_v, height)
+    correct(0, INNER[0], flat, u_new, v_new, u_all, v_all, flow_u, flow_v)
+    correct(INNER[0], CORE[0], flat, u_done, v_done, u_all, v_all, flow_u, flow_v)
+    correct(CORE[1], INNER[1], flat, u_done, v_done, u_all, v_all, flow_u, flow_v)
+    correct(INNER[1], EXT // 8, flat, u_new, v_new, u_all, v_all, flow_u, flow_v)
+
+    for t in range(2):
+        for k in range(LEVELS):
+            for at in (8 * CORE[0], 8 * CORE[1] - 8):
+                rows = pl.ds(PAD + at, 8)
+                u_all[k, t, rows, :] = u_next[k, t, rows, :]
+                v_all[k, t, rows, :] = v_next[k, t, rows, :]
+        flow_u[0, t, core, :] = later[0, t, core, :]
+        flow_v[0, t, core, :] = later[1, t, core, :]
+        height[t, core, :] = later[2, t, core, :]
+        for i, which in enumerate(SUMS):
+            flat[which, t, core, :] = later_sums[i, t, core, :]
+    ghosts()
+    lax.fori_loop(1, CORE[0], tend, 0)
+    lax.fori_loop(CORE[1], jnp.where(top, EXT // 8, EXT // 8 - 2), tend, 0)
+    substeps(CHUNKS, top, flat, flow_u, flow_v, height)
+    correct(OWN // 8, CORE[0], flat, u_new, v_new, u_out, v_out, None, None)
+    correct(CORE[0], CORE[1], flat, u_done, v_done, u_out, v_out, None, None)
+    correct(CORE[1], (OWN + ROWS) // 8, flat, u_new, v_new, u_out, v_out, None, None)
     h_out[...] = height[0, pl.ds(PAD + OWN, ROWS), :]
 
 
@@ -555,12 +609,14 @@
 
     turn_centre, turn_face = turning(lax.axis_index("lat"))
     levels, pair, single = (LEVELS, 2, TALL, LANES), (2, 2, TALL, LANES), (2, TALL, LANES)
-    shapes = [levels] * 5 + [(len(SUMS), 2, TALL, LANES), single, single, (1, 2, TALL, LANES), (1, 2, TALL, LANES), single]
+    four, three = (4, 2, TALL, LANES), (3, 2, TALL, LANES)
+    shapes = [levels] * 7 + [four, four, single, single, pair, single, three]
     done = pl.pallas_call(
         inner_rows,
         out_shape=tuple(jax.ShapeDtypeStruct(shape, f32) for shape in shapes),
-        scratch_shapes=[pltpu.VMEM((16, 2, TALL, LANES), f32)],
-        compiler_params=params,
+        scratch_shapes=[pltpu.VMEM((16, 2, TALL, LANES), f32)]
+        + [pltpu.VMEM(pair, f32), pltpu.VMEM(pair, f32), pltpu.VMEM(single, f32)],
+        compiler_params=pltpu.CompilerParams(vmem_limit_bytes=12 * 1024 * 1024),
         cost_estimate=pl.CostEstimate(flops=40000000, bytes_accessed=12000000, transcendentals=0),
     )(own, east_a, east_b, turn_centre, turn_face)
     return pl.pallas_call(

time: 50.9 us -> 48.9 us (0.961)
  waiting for transfers between devices: 17.4 us -> 13.9 us
  Pallas kernels: 19.6 us -> 21.1 us
    pallas_call x1, Pallas kernels: 3.48 us -> 6.97 us  [shards(): pl.pallas_call(inner_rows, out_shape=tuple((jax.ShapeDtypeStruct(shape, f...]
    ppermute x1, waiting for transfers between devices: 12.2 us -> 8.73 us  [shards(): north_b = lax.ppermute(rows_b, ('lon', 'lat'), lat_second)]
    pallas_call x1, Pallas kernels: 11.3 us -> 9.28 us  [shards(): pl.pallas_call(ocean_steps, out_shape=(jax.ShapeDtypeStruct(level_block,...]
  transfers between devices with their start and end apart: 4 -> 4, of which waited for: 2 -> 2; matrix products, arithmetic and copies ran while one was open for 0% -> 0% of each run, Pallas kernels for 8% -> 15%
where the time goes in v3:
time: 48.9 us; the launch traced here: 48.8 us
  Pallas kernels  21.1 us (43%)
  waiting for transfers between devices  13.9 us (28%)
  starting transfers between devices  12.8 us (26%)
  between operations  0.78 us (2%)
    pallas_call x1, Pallas kernels, shards(): pl.pallas_call(ocean_steps, out_shape=(jax.ShapeDtypeStruct(level_block,...  9.28 us
    ppermute x1, waiting for transfers between devices, shards(): north_b = lax.ppermute(rows_b, ('lon', 'lat'), lat_second)  8.73 us
    ppermute x1, starting transfers between devices, shards(): east_b = lax.ppermute(pack_b, 'lon', lon_second)  7.3 us
    pallas_call x1, Pallas kernels, shards(): pl.pallas_call(inner_rows, out_shape=tuple((jax.ShapeDtypeStruct(shape, f...  6.97 us
    ppermute x1, waiting for transfers between devices, shards(): east_b = lax.ppermute(pack_b, 'lon', lon_second)  5.13 us
    ppermute x1, starting transfers between devices, shards(): north_b = lax.ppermute(rows_b, ('lon', 'lat'), lat_second)  3.73 us
    pallas_call x1, Pallas kernels, shards(): pl.pallas_call(strips, out_shape=(jax.ShapeDtypeStruct((PACKS, ROWS, LANE...  3.42 us
    ppermute x1, starting transfers between devices, shards(): east_a = lax.ppermute(pack_a, 'lon', lon_first)  1.72 us
  transfers between devices with their start and end apart: 4, of which 2 were waited for; matrix products, arithmetic and copies ran while one was open for 0% of the time, Pallas kernels for 15%

profile of v3, /device:TPU:7, one launch (start us, length us, event | category | flops | bytes accessed | tf_op | source)
XLA Modules:
  0.0 48.8 jit_solution(3959904131524133154)
XLA Ops:
  0.6 0.0 copy-start.3
  0.6 0.0 copy-start.5
  0.7 0.0 copy-start
  0.7 0.0 copy-start.1
  0.7 0.0 copy-start.2
  0.7 0.0 copy-start.4
  0.7 3.4 %shard_map.86 = (f32[5,96,128]{2,1,0:T(8,128)}, f32[5,96,128]{2,1,0:T(8,128)}) custom-call(f32[12,96,128]{2,1,0:T(8,128)} %u_far.1, f32[12,96,128]{2,1,0:T(8,128)} %v_far.1, f32[12,96,128]{2,1,0:T(8,128)} %d_far.1, f32[96,128]{1,0:T(8,128)} %s_far.1, s32[12,96,128]{2,1,0:T(8,128)} %m_far.1, s32[96,128]{1,0:T(8,128)} %b_far.1), custom_call_target="tpu_custom_call" | custom-call | tf_op jit(solution)/shard_map/pallas_call | solution.py:574
  4.1 1.7 %collective-permute-start = (f32[5,96,128]{2,1,0:T(8,128)}, f32[5,96,128]{2,1,0:T(8,128)S(1)}, u32[]{:S(2)}, u32[]{:S(2)}) collective-permute-start(f32[5,96,128]{2,1,0:T(8,128)} %get-tuple-element.21), channel_id=1, source_target_pairs={{0,16},{16,0},{32,48},{48,32},{64,80},{80,64},{96,112},{112,96},{1... | collective-permute-start | bytes 737288 | tf_op jit(solution)/shard_map/ppermute | solution.py:584
  5.8 7.3 %collective-permute-start.1 = (f32[5,96,128]{2,1,0:T(8,128)}, f32[5,96,128]{2,1,0:T(8,128)S(1)}, u32[]{:S(2)}, u32[]{:S(2)}) collective-permute-start(f32[5,96,128]{2,1,0:T(8,128)} %get-tuple-element.22), channel_id=1, source_target_pairs={{0,240},{16,32},{32,16},{48,64},{64,48},{80,96},{96,80},{112,128},... | collective-permute-start | bytes 737288 | tf_op jit(solution)/shard_map/ppermute | solution.py:585
  13.1 0.0 copy-done.5
  13.2 0.0 copy-done.1
  13.2 0.4 shard_map.85.low_own.top_own.own_ref
  13.6 0.0 collective-permute-done.low_a.top_a.ea_ref
  13.6 5.1 %collective-permute-done.1.low_b.top_b.eb_ref = f32[5,96,128]{2,1,0:T(8,128)S(1)} collective-permute-done((f32[5,96,128]{2,1,0:T(8,128)}, f32[5,96,128]{2,1,0:T(8,128)S(1)}, u32[]{:S(2)}, u32[]{:S(2)}) %collective-permute-start.1) | collective-permute-done | bytes 245792 | tf_op jit(solution)/shard_map/ppermute | solution.py:585
  18.7 1.0 %shard_map.87 = (f32[784,128]{1,0:T(8,128)}, f32[888,128]{1,0:T(8,128)}) custom-call(f32[39,96,128]{2,1,0:T(8,128)S(1)} %shard_map.85.low_own.top_own.own_ref, f32[5,96,128]{2,1,0:T(8,128)S(1)} %collective-permute-done.low_a.top_a.ea_ref, f32[5,96,128]{2,1,0:T(8,128)S(1)} %collective-permute-done.1.low_b.top_b.eb_ref, ...), custom_call_target="tpu_custom_call" | custom-call | tf_op jit(solution)/shard_map/pallas_call | solution.py:595
  19.7 3.7 %collective-permute-start.3 = (f32[888,128]{1,0:T(8,128)}, f32[888,128]{1,0:T(8,128)S(1)}, u32[]{:S(2)}, u32[]{:S(2)}) collective-permute-start(f32[888,128]{1,0:T(8,128)} %get-tuple-element.24), channel_id=1, source_target_pairs={{1,2},{17,18},{33,34},{49,50},{65,66},{81,82},{97,98},{113,114},{1... | collective-permute-start | bytes 1363976 | tf_op jit(solution)/shard_map/ppermute | solution.py:607
  23.4 0.1 collective-permute-start.2
  23.5 0.1 select_multiply_fusion
  23.6 0.1 broadcast_in_dim.22.ft_ref
  23.7 0.1 broadcast_in_dim.23.fv_ref
  23.8 7.0 %shard_map.88 = (f32[12,2,152,128]{3,2,1,0:T(8,128)S(1)}, f32[12,2,152,128]{3,2,1,0:T(8,128)S(1)}, f32[12,2,152,128]{3,2,1,0:T(8,128)S(1)}, f32[12,2,152,128]{3,...) custom-call(f32[39,96,128]{2,1,0:T(8,128)S(1)} %shard_map.85.low_own, ...), custom_call_target="tpu_custom_call" | custom-call | flops 40000000 | bytes 12000000 | tf_op jit(solution)/shard_map/pallas_call | solution.py:614
  30.7 0.0 collective-permute-done.2.na_ref
  30.8 8.7 %collective-permute-done.3.nb_ref = f32[888,128]{1,0:T(8,128)S(1)} collective-permute-done((f32[888,128]{1,0:T(8,128)}, f32[888,128]{1,0:T(8,128)S(1)}, u32[]{:S(2)}, u32[]{:S(2)}) %collective-permute-start.3) | collective-permute-done | bytes 454688 | tf_op jit(solution)/shard_map/ppermute | solution.py:607
  39.5 9.3 %shard_map.89 = (f32[12,96,128]{2,1,0:T(8,128)}, f32[12,96,128]{2,1,0:T(8,128)}, f32[96,128]{1,0:T(8,128)}) custom-call(f32[784,128]{1,0:T(8,128)S(1)} %collective-permute-done.2.na_ref, f32[888,128]{1,0:T(8,128)S(1)} %collective-permute-done.3.nb_ref, f32[152,128]{1,0:T(8,128)S(1)} %broadcast_in_dim.22.ft_ref, f32[152,128]{1,0:T(8,128)S(1)} %broadcast_in_dim.23.fv_ref, ...), custom_call_target="tpu_custom_call" | custom-call | tf_op jit(solution)/shard_map/pallas_call | solution.py:622
  (4 shorter events, 0.0 us)
Async XLA Ops:
  0.6 12.5 %copy-start.3 = (s32[12,96,128]{2,1,0:T(8,128)S(1)}, s32[12,96,128]{2,1,0:T(8,128)}, u32[]{:S(2)}) copy-start(s32[12,96,128]{2,1,0:T(8,128)} %m_far.1) | copy-start | bytes 1769476
  0.6 12.5 %copy-start.5 = (s32[96,128]{1,0:T(8,128)S(1)}, s32[96,128]{1,0:T(8,128)}, u32[]{:S(2)}) copy-start(s32[96,128]{1,0:T(8,128)} %b_far.1) | copy-start | bytes 147460
  0.7 12.5 %copy-start = (f32[12,96,128]{2,1,0:T(8,128)S(1)}, f32[12,96,128]{2,1,0:T(8,128)}, u32[]{:S(2)}) copy-start(f32[12,96,128]{2,1,0:T(8,128)} %u_far.1) | copy-start | bytes 1769476
  0.7 12.5 %copy-start.1 = (f32[12,96,128]{2,1,0:T(8,128)S(1)}, f32[12,96,128]{2,1,0:T(8,128)}, u32[]{:S(2)}) copy-start(f32[12,96,128]{2,1,0:T(8,128)} %v_far.1) | copy-start | bytes 1769476
  0.7 12.5 %copy-start.2 = (f32[12,96,128]{2,1,0:T(8,128)S(1)}, f32[12,96,128]{2,1,0:T(8,128)}, u32[]{:S(2)}) copy-start(f32[12,96,128]{2,1,0:T(8,128)} %d_far.1) | copy-start | bytes 1769476
  0.7 12.5 %copy-start.4 = (f32[96,128]{1,0:T(8,128)S(1)}, f32[96,128]{1,0:T(8,128)}, u32[]{:S(2)}) copy-start(f32[96,128]{1,0:T(8,128)} %s_far.1) | copy-start | bytes 147460
  4.1 9.5 %collective-permute-start = (f32[5,96,128]{2,1,0:T(8,128)}, f32[5,96,128]{2,1,0:T(8,128)S(1)}, u32[]{:S(2)}, u32[]{:S(2)}) collective-permute-start(f32[5,96,128]{2,1,0:T(8,128)} %get-tuple-element.21), channel_id=1, source_target_pairs={{0,16},{16,0},{32,48},{48,32},{64,80},{80,64},{96,112},{112,96},{1... | collective-permute-start | bytes 737288 | tf_op jit(solution)/shard_map/ppermute | solution.py:584
  5.8 12.9 %collective-permute-start.1 = (f32[5,96,128]{2,1,0:T(8,128)}, f32[5,96,128]{2,1,0:T(8,128)S(1)}, u32[]{:S(2)}, u32[]{:S(2)}) collective-permute-start(f32[5,96,128]{2,1,0:T(8,128)} %get-tuple-element.22), channel_id=1, source_target_pairs={{0,240},{16,32},{32,16},{48,64},{64,48},{80,96},{96,80},{112,128},... | collective-permute-start | bytes 737288 | tf_op jit(solution)/shard_map/ppermute | solution.py:585
  19.7 19.8 %collective-permute-start.3 = (f32[888,128]{1,0:T(8,128)}, f32[888,128]{1,0:T(8,128)S(1)}, u32[]{:S(2)}, u32[]{:S(2)}) collective-permute-start(f32[888,128]{1,0:T(8,128)} %get-tuple-element.24), channel_id=1, source_target_pairs={{1,2},{17,18},{33,34},{49,50},{65,66},{81,82},{97,98},{113,114},{1... | collective-permute-start | bytes 1363976 | tf_op jit(solution)/shard_map/ppermute | solution.py:607
  23.4 7.3 %collective-permute-start.2 = (f32[784,128]{1,0:T(8,128)}, f32[784,128]{1,0:T(8,128)S(1)}, u32[]{:S(2)}, u32[]{:S(2)}) collective-permute-start(f32[784,128]{1,0:T(8,128)} %get-tuple-element.23), channel_id=1, source_target_pairs={{0,1},{16,17},{32,33},{48,49},{64,65},{80,81},{96,97},{112,113},{1... | collective-permute-start | bytes 1204232 | tf_op jit(solution)/shard_map/ppermute | solution.py:608

commit v4 on v3

--- a/solution.py
+++ b/solution.py
@@ -132,9 +132,7 @@
 (BED, FROM, UP_U, LO_U, UP_V, C_U, F_U, G_U, C_V, F_V, G_V, SUM_U, SUM_V, NEW_U, NEW_V, SEA) = range(16)
 INNER = (3, 12)
 CORE = (4, 11)
-CORE_ROWS = (8 * CORE[0], 8 * (CORE[1] - CORE[0]))
-INNER_CHUNKS = ((24, 32), (56, 40))
-OUTER_CHUNKS = ((0, 40), (80, 24), (104, 32))
+CORE_ROWS = 88
 SUMS = (G_U, G_V, NEW_U, NEW_V)
 
 
@@ -283,8 +281,7 @@
 def substeps(chunks, top, flat, flow_u, flow_v, height):
     for which in (SUM_U, SUM_V):
         for t in range(2):
-            for at, n in chunks:
-                flat[which, t, pl.ds(PAD + at, n), :] = jnp.zeros((n, LANES), jnp.float32)
+            flat[which, t, pl.ds(PAD, EXT), :] = jnp.zeros((EXT, LANES), jnp.float32)
 
     def two(turn, carry):
         substep(0, 1, chunks, top, flat, flow_u, flow_v, height)
@@ -326,10 +323,11 @@
 
 
 def inner_rows(
-    own_ref, ea_ref, eb_ref, ft_ref, fv_ref,
+    own_ref, ea_ref, eb_ref, na_ref, ft_ref, fv_ref,
     u_all, v_all, p_all, u_new, v_new, u_next, v_next, sums, later_sums, bed, start, flows, height_in, later,
     flat, flow_u, flow_v, height,
 ):
+    even_lat = lax.rem(lax.axis_index("lat"), 2) == 0
     even_lon = lax.rem(lax.axis_index("lon"), 2) == 0
     place = [u_all.at[k] for k in range(LEVELS)] + [v_all.at[k] for k in range(LEVELS)]
     place += [p_all.at[k] for k in range(LEVELS)] + [flat.at[BED], flat.at[FROM], height]
@@ -341,8 +339,24 @@
             for p, tile in zip(planes_of(pack), tiles):
                 place[p][0, pl.ds(PAD + OWN + at, 32), :] = own_ref[p, pl.ds(at, 32), :]
                 place[p][1, pl.ds(PAD + OWN + at, 32), :] = tile
-    faces(OWN, 48, flat, ft_ref, fv_ref, False)
-    faces(OWN + 48, 40, flat, ft_ref, fv_ref, False)
+        at = pl.multiple_of(jnp.where(even_lat, PAD + OWN + ROWS, PAD), 8)
+        a, b = na_ref[pl.ds((PLANES + pack) * HALO, HALO), :], na_ref[pl.ds((PLANES + PACKS + pack) * HALO, HALO), :]
+        east, west = jnp.where(even_lon, a, b), jnp.where(even_lon, b, a)
+        tiles = [(na_ref[pl.ds(p * HALO, HALO), :], beside(east, west, p)) for p in planes_of(pack)]
+        for p, (t0, t1) in zip(planes_of(pack), tiles):
+            place[p][0, pl.ds(at, HALO), :] = t0
+            place[p][1, pl.ds(at, HALO), :] = t1
+            for t in range(2):
+                place[p][t, pl.ds(0, PAD), :] = jnp.full((PAD, LANES), beyond(p), jnp.float32)
+                place[p][t, pl.ds(TALL - 16, 16), :] = jnp.full((16, LANES), beyond(p), jnp.float32)
+    for at, n in CHUNKS:
+        faces(at, n, flat, ft_ref, fv_ref, False)
+    for t in range(2):
+        for flow in (flow_u, flow_v):
+            for now in range(2):
+                flow[now, t, :, :] = jnp.zeros((TALL, LANES), jnp.float32)
+        for which in (G_U, G_V):
+            flat[which, t, pl.ds(PAD, EXT), :] = jnp.zeros((EXT, LANES), jnp.float32)
 
     def first(r, carry):
         mask_rows(r, flat, u_all, v_all, flow_u, flow_v)
@@ -352,31 +366,31 @@
         tendencies(r, flat, ft_ref, fv_ref, u_all, v_all, p_all, u_new, v_new)
         return carry
 
-    lax.fori_loop(INNER[0] - 1, INNER[1] + 1, first, 0)
-    lax.fori_loop(INNER[0], INNER[1], second, 0)
+    tiles = EXT // 8
+    lax.fori_loop(jnp.where(even_lat, INNER[0] - 1, 0), jnp.where(even_lat, tiles, INNER[1] + 1), first, 0)
+    begin, end = jnp.where(even_lat, INNER[0], 0), jnp.where(even_lat, tiles - 1, INNER[1])
+    lax.fori_loop(begin, end, second, 0)
     own = pl.ds(PAD + OWN, ROWS)
     inner = pl.ds(PAD + 8 * INNER[0], 8 * (INNER[1] - INNER[0]))
     masked = pl.ds(PAD + 8 * (INNER[0] - 1), 8 * (INNER[1] - INNER[0] + 2))
-    core = pl.ds(PAD + CORE_ROWS[0], CORE_ROWS[1])
-    for t in range(2):
-        bed[t, own, :] = flat[BED, t, own, :]
-        start[t, own, :] = flat[FROM, t, own, :]
+    core = pl.ds(pl.multiple_of(jnp.where(even_lat, PAD + 8 * CORE[0], PAD), 8), CORE_ROWS)
+    for t in range(2):
+        bed[t, :, :] = flat[BED, t, :, :]
+        start[t, :, :] = flat[FROM, t, :, :]
         height_in[t, own, :] = height[t, own, :]
         flows[0, t, masked, :] = flow_u[0, t, masked, :]
         flows[1, t, masked, :] = flow_v[0, t, masked, :]
         for i, which in enumerate(SUMS):
             sums[i, t, inner, :] = flat[which, t, inner, :]
-        for flow in (flow_u, flow_v):
-            flow[1, t, pl.ds(PAD + 8 * INNER[0] - 8, 8), :] = jnp.zeros((8, LANES), jnp.float32)
-            flow[1, t, pl.ds(PAD + 8 * INNER[1], 8), :] = jnp.zeros((8, LANES), jnp.float32)
-    substeps(INNER_CHUNKS, None, flat, flow_u, flow_v, height)
-    correct(INNER[0], INNER[1], flat, u_new, v_new, u_next, v_next, flow_u, flow_v)
+    base = pl.multiple_of(8 * begin, 8)
+    substeps(((base, 32), (base + 32, 32), (base + 64, 40)), None, flat, flow_u, flow_v, height)
+    correct(begin, end, flat, u_new, v_new, u_next, v_next, flow_u, flow_v)
 
     def third(r, carry):
         tendencies(r, flat, ft_ref, fv_ref, u_next, v_next, p_all, u_new, v_new)
         return carry
 
-    lax.fori_loop(CORE[0], CORE[1], third, 0)
+    lax.fori_loop(jnp.where(even_lat, CORE[0], 1), jnp.where(even_lat, tiles - 2, CORE[1]), third, 0)
     for t in range(2):
         later[0, t, core, :] = flow_u[0, t, core, :]
         later[1, t, core, :] = flow_v[0, t, core, :]
@@ -386,7 +400,7 @@
 
 
 def ocean_steps(
-    na_ref, nb_ref, ft_ref, fv_ref,
+    nb_ref, ft_ref, fv_ref,
     u_in, v_in, p_in, u_done, v_done, u_next, v_next, sums, later_sums, bed, start, flows, height_in, later,
     u_out, v_out, h_out,
     u_all, v_all, p_all, u_new, v_new,
@@ -399,16 +413,10 @@
     place = [u_all.at[k] for k in range(LEVELS)] + [v_all.at[k] for k in range(LEVELS)]
     place += [p_all.at[k] for k in range(LEVELS)] + [flat.at[BED], flat.at[FROM], height]
 
-    def north_rows(p):
-        return jnp.where(even_lat, na_ref[pl.ds(p * HALO, HALO), :], nb_ref[pl.ds(p * FOLD, HALO), :])
-
-    def south_rows(p):
-        return jnp.where(even_lat, nb_ref[pl.ds(p * FOLD + FOLD - HALO, HALO), :], na_ref[pl.ds(p * HALO, HALO), :])
-
     own = pl.ds(PAD + OWN, ROWS)
     low = pl.ds(PAD + OWN, 8 * (CORE[0] + 1) - OWN)
     high = pl.ds(PAD + 8 * (CORE[1] - 1), OWN + ROWS - 8 * (CORE[1] - 1))
-    core = pl.ds(PAD + CORE_ROWS[0], CORE_ROWS[1])
+    core = pl.ds(pl.multiple_of(jnp.where(even_lat, PAD + 8 * CORE[0], PAD), 8), CORE_ROWS)
     inner = pl.ds(PAD + 8 * INNER[0], 8 * (INNER[1] - INNER[0]))
     masked = pl.ds(PAD + 8 * (INNER[0] - 1), 8 * (INNER[1] - INNER[0] + 2))
     for t in range(2):
@@ -417,8 +425,11 @@
                 p_all[k, t, rows, :] = p_in[k, t, rows, :]
                 u_all[k, t, rows, :] = u_in[k, t, rows, :]
                 v_all[k, t, rows, :] = v_in[k, t, rows, :]
-        flat[BED, t, own, :] = bed[t, own, :]
-        flat[FROM, t, own, :] = start[t, own, :]
+        flat[BED, t, :, :] = bed[t, :, :]
+        flat[FROM, t, :, :] = start[t, :, :]
+        for flow in (flow_u, flow_v):
+            for now in range(2):
+                flow[now, t, :, :] = jnp.zeros((TALL, LANES), jnp.float32)
         height[t, own, :] = height_in[t, own, :]
         flow_u[0, t, masked, :] = flows[0, t, masked, :]
         flow_v[0, t, masked, :] = flows[1, t, masked, :]
@@ -427,15 +438,18 @@
             flat[which, t, pl.ds(PAD + EXT - 8, 8), :] = jnp.zeros((8, LANES), jnp.float32)
 
     edge, after = pl.ds(0, PAD), pl.ds(PAD + OWN + ROWS + HALO, 16)
+    at = pl.multiple_of(jnp.where(even_lat, PAD, PAD + OWN + ROWS), 8)
+
+    def rows_of(p):
+        return jnp.where(even_lat, nb_ref[pl.ds(p * FOLD + FOLD - HALO, HALO), :], nb_ref[pl.ds(p * FOLD, HALO), :])
+
     for pack in range(PACKS):
-        pa, pb = PLANES + pack, PLANES + PACKS + pack
-        for rows, at in ((south_rows, PAD), (north_rows, PAD + OWN + ROWS)):
-            a, b = rows(pa), rows(pb)
-            east, west = jnp.where(even_lon, a, b), jnp.where(even_lon, b, a)
-            tiles = [(rows(p), beside(east, west, p)) for p in planes_of(pack)]
-            for p, (t0, t1) in zip(planes_of(pack), tiles):
-                place[p][0, pl.ds(at, HALO), :] = t0
-                place[p][1, pl.ds(at, HALO), :] = t1
+        a, b = rows_of(PLANES + pack), rows_of(PLANES + PACKS + pack)
+        east, west = jnp.where(even_lon, a, b), jnp.where(even_lon, b, a)
+        tiles = [(rows_of(p), beside(east, west, p)) for p in planes_of(pack)]
+        for p, (t0, t1) in zip(planes_of(pack), tiles):
+            place[p][0, pl.ds(at, HALO), :] = t0
+            place[p][1, pl.ds(at, HALO), :] = t1
         for p in planes_of(pack):
             for t in range(2):
                 place[p][t, edge, :] = jnp.full((PAD, LANES), beyond(p), jnp.float32)
@@ -470,18 +484,12 @@
     fold_ghosts(flat.at[BED], top)
     for at, n in CHUNKS:
         faces(at, n, flat, ft_ref, fv_ref, top)
-    for flow in (flow_u, flow_v):
-        for now in range(2):
-            for t in range(2):
-                flow[now, t, edge, :] = jnp.zeros((PAD, LANES), jnp.float32)
-                flow[now, t, pl.ds(PAD + EXT, PAD), :] = jnp.zeros((PAD, LANES), jnp.float32)
-
     def mask_first(r, carry):
         mask_rows(r, flat, u_all, v_all, flow_u, flow_v)
         return carry
 
-    lax.fori_loop(0, INNER[0] - 1, mask_first, 0)
-    lax.fori_loop(INNER[1] + 1, EXT // 8, mask_first, 0)
+    tiles = EXT // 8
+    lax.fori_loop(jnp.where(even_lat, 0, INNER[1] + 1), jnp.where(even_lat, INNER[0] - 1, tiles), mask_first, 0)
 
     def ghosts():
         for k in range(LEVELS):
@@ -496,17 +504,13 @@
     for k in range(LEVELS):
         fold_ghosts(p_all.at[k], top)
     ghosts()
-    lax.fori_loop(0, INNER[0], tend, 0)
-    lax.fori_loop(INNER[1], jnp.where(top, EXT // 8, EXT // 8 - 1), tend, 0)
-    for flow in (flow_u, flow_v):
-        for t in range(2):
-            for at in (40, 72):
-                flow[1, t, pl.ds(PAD + at, 8), :] = jnp.zeros((8, LANES), jnp.float32)
-    substeps(OUTER_CHUNKS, top, flat, flow_u, flow_v, height)
-    correct(0, INNER[0], flat, u_new, v_new, u_all, v_all, flow_u, flow_v)
-    correct(INNER[0], CORE[0], flat, u_done, v_done, u_all, v_all, flow_u, flow_v)
-    correct(CORE[1], INNER[1], flat, u_done, v_done, u_all, v_all, flow_u, flow_v)
-    correct(INNER[1], EXT // 8, flat, u_new, v_new, u_all, v_all, flow_u, flow_v)
+    first, end = jnp.where(even_lat, 0, INNER[1]), jnp.where(even_lat, INNER[0], jnp.where(top, tiles, tiles - 1))
+    lax.fori_loop(first, end, tend, 0)
+    base = pl.multiple_of(jnp.where(even_lat, 0, 8 * CORE[1] - 8), 8)
+    substeps(((base, 24), (base + 24, 32)), top, flat, flow_u, flow_v, height)
+    correct(first, jnp.where(even_lat, INNER[0], tiles), flat, u_new, v_new, u_all, v_all, flow_u, flow_v)
+    between = jnp.where(even_lat, INNER[0], CORE[1])
+    correct(between, between + 1, flat, u_done, v_done, u_all, v_all, flow_u, flow_v)
 
     for t in range(2):
         for k in range(LEVELS):
@@ -520,12 +524,14 @@
         for i, which in enumerate(SUMS):
             flat[which, t, core, :] = later_sums[i, t, core, :]
     ghosts()
-    lax.fori_loop(1, CORE[0], tend, 0)
-    lax.fori_loop(CORE[1], jnp.where(top, EXT // 8, EXT // 8 - 2), tend, 0)
+    end = jnp.where(even_lat, CORE[0], jnp.where(top, tiles, tiles - 2))
+    lax.fori_loop(jnp.where(even_lat, 1, CORE[1]), end, tend, 0)
     substeps(CHUNKS, top, flat, flow_u, flow_v, height)
-    correct(OWN // 8, CORE[0], flat, u_new, v_new, u_out, v_out, None, None)
-    correct(CORE[0], CORE[1], flat, u_done, v_done, u_out, v_out, None, None)
-    correct(CORE[1], (OWN + ROWS) // 8, flat, u_new, v_new, u_out, v_out, None, None)
+    low, high = OWN // 8, (OWN + ROWS) // 8
+    here = jnp.where(even_lat, low, CORE[1]), jnp.where(even_lat, CORE[0], high)
+    done = jnp.where(even_lat, CORE[0], low), jnp.where(even_lat, high, CORE[1])
+    correct(*here, flat, u_new, v_new, u_out, v_out, None, None)
+    correct(*done, flat, u_done, v_done, u_out, v_out, None, None)
     h_out[...] = height[0, pl.ds(PAD + OWN, ROWS), :]
 
 
@@ -618,7 +624,7 @@
         + [pltpu.VMEM(pair, f32), pltpu.VMEM(pair, f32), pltpu.VMEM(single, f32)],
         compiler_params=pltpu.CompilerParams(vmem_limit_bytes=12 * 1024 * 1024),
         cost_estimate=pl.CostEstimate(flops=40000000, bytes_accessed=12000000, transcendentals=0),
-    )(own, east_a, east_b, turn_centre, turn_face)
+    )(own, east_a, east_b, north_a, turn_centre, turn_face)
     return pl.pallas_call(
         ocean_steps,
         out_shape=(
@@ -630,7 +636,7 @@
         + [pltpu.VMEM((16, 2, TALL, LANES), f32)]
         + [pltpu.VMEM(pair, f32), pltpu.VMEM(pair, f32), pltpu.VMEM(single, f32)],
         compiler_params=params,
-    )(north_a, north_b, turn_centre, turn_face, *done)
+    )(north_b, turn_centre, turn_face, *done)
 
 
 def solution(mesh):

time: 48.9 us -> 47.2 us (0.965)
  waiting for transfers between devices: 13.9 us -> 11.9 us
    ppermute x1, waiting for transfers between devices: 8.73 us -> 4.9 us  [shards(): north_b = lax.ppermute(rows_b, ('lon', 'lat'), lat_second)]
    pallas_call x1, Pallas kernels: 6.97 us -> 8.95 us  [shards(): pl.pallas_call(inner_rows, out_shape=tuple((jax.ShapeDtypeStruct(shape, f...]
    ppermute x1, waiting for transfers between devices: 0.01 us -> 1.86 us  [shards(): north_a = lax.ppermute(rows_a, ('lon', 'lat'), lat_first)]
    pallas_call x1, Pallas kernels: 9.28 us -> 7.59 us  [shards(): pl.pallas_call(ocean_steps, out_shape=(jax.ShapeDtypeStruct(level_block,...]
  transfers between devices with their start and end apart: 4 -> 4, of which waited for: 2 -> 3; matrix products, arithmetic and copies ran while one was open for 0% -> 0% of each run, Pallas kernels for 15% -> 20%
where the time goes in v4:
time: 47.2 us; the launch traced here: 47.1 us
  Pallas kernels  21.3 us (45%)
  starting transfers between devices  12.8 us (27%)
  waiting for transfers between devices  11.9 us (25%)
  between operations  0.77 us (2%)
    pallas_call x1, Pallas kernels, shards(): pl.pallas_call(inner_rows, out_shape=tuple((jax.ShapeDtypeStruct(shape, f...  8.95 us
    pallas_call x1, Pallas kernels, shards(): pl.pallas_call(ocean_steps, out_shape=(jax.ShapeDtypeStruct(level_block,...  7.59 us
    ppermute x1, starting transfers between devices, shards(): east_b = lax.ppermute(pack_b, 'lon', lon_second)  7.3 us
    ppermute x1, waiting for transfers between devices, shards(): east_b = lax.ppermute(pack_b, 'lon', lon_second)  5.13 us
    ppermute x1, waiting for transfers between devices, shards(): north_b = lax.ppermute(rows_b, ('lon', 'lat'), lat_second)  4.9 us
    ppermute x1, starting transfers between devices, shards(): north_b = lax.ppermute(rows_b, ('lon', 'lat'), lat_second)  3.73 us
    pallas_call x1, Pallas kernels, shards(): pl.pallas_call(strips, out_shape=(jax.ShapeDtypeStruct((PACKS, ROWS, LANE...  3.42 us
    ppermute x1, waiting for transfers between devices, shards(): north_a = lax.ppermute(rows_a, ('lon', 'lat'), lat_first)  1.86 us
  transfers between devices with their start and end apart: 4, of which 3 were waited for; matrix products, arithmetic and copies ran while one was open for 0% of the time, Pallas kernels for 20%

profile of v4, /device:TPU:7, one launch (start us, length us, event | category | flops | bytes accessed | tf_op | source)
XLA Modules:
  0.0 47.1 jit_solution(14563755517219478751)
XLA Ops:
  0.6 0.0 copy-start.5
  0.6 0.0 copy-start.3
  0.7 0.0 copy-start.4
  0.7 0.0 copy-start.2
  0.7 0.0 copy-start.1
  0.7 0.0 copy-start
  0.7 3.4 %shard_map.86 = (f32[5,96,128]{2,1,0:T(8,128)}, f32[5,96,128]{2,1,0:T(8,128)}) custom-call(f32[12,96,128]{2,1,0:T(8,128)} %u_far.1, f32[12,96,128]{2,1,0:T(8,128)} %v_far.1, f32[12,96,128]{2,1,0:T(8,128)} %d_far.1, f32[96,128]{1,0:T(8,128)} %s_far.1, s32[12,96,128]{2,1,0:T(8,128)} %m_far.1, s32[96,128]{1,0:T(8,128)} %b_far.1), custom_call_target="tpu_custom_call" | custom-call | tf_op jit(solution)/shard_map/pallas_call | solution.py:580
  4.1 1.7 %collective-permute-start = (f32[5,96,128]{2,1,0:T(8,128)}, f32[5,96,128]{2,1,0:T(8,128)S(1)}, u32[]{:S(2)}, u32[]{:S(2)}) collective-permute-start(f32[5,96,128]{2,1,0:T(8,128)} %get-tuple-element.21), channel_id=1, source_target_pairs={{0,16},{16,0},{32,48},{48,32},{64,80},{80,64},{96,112},{112,96},{1... | collective-permute-start | bytes 737288 | tf_op jit(solution)/shard_map/ppermute | solution.py:590
  5.8 7.3 %collective-permute-start.1 = (f32[5,96,128]{2,1,0:T(8,128)}, f32[5,96,128]{2,1,0:T(8,128)S(1)}, u32[]{:S(2)}, u32[]{:S(2)}) collective-permute-start(f32[5,96,128]{2,1,0:T(8,128)} %get-tuple-element.22), channel_id=1, source_target_pairs={{0,240},{16,32},{32,16},{48,64},{64,48},{80,96},{96,80},{112,128},... | collective-permute-start | bytes 737288 | tf_op jit(solution)/shard_map/ppermute | solution.py:591
  13.1 0.0 copy-done.3
  13.2 0.0 copy-done.2
  13.2 0.4 shard_map.85.low_own.top_own.own_ref
  13.6 0.0 collective-permute-done.low_a.top_a.ea_ref
  13.6 5.1 %collective-permute-done.1.low_b.top_b.eb_ref = f32[5,96,128]{2,1,0:T(8,128)S(1)} collective-permute-done((f32[5,96,128]{2,1,0:T(8,128)}, f32[5,96,128]{2,1,0:T(8,128)S(1)}, u32[]{:S(2)}, u32[]{:S(2)}) %collective-permute-start.1) | collective-permute-done | bytes 245792 | tf_op jit(solution)/shard_map/ppermute | solution.py:591
  18.7 1.0 %shard_map.87 = (f32[784,128]{1,0:T(8,128)}, f32[888,128]{1,0:T(8,128)}) custom-call(f32[39,96,128]{2,1,0:T(8,128)S(1)} %shard_map.85.low_own.top_own.own_ref, f32[5,96,128]{2,1,0:T(8,128)S(1)} %collective-permute-done.low_a.top_a.ea_ref, f32[5,96,128]{2,1,0:T(8,128)S(1)} %collective-permute-done.1.low_b.top_b.eb_ref, ...), custom_call_target="tpu_custom_call" | custom-call | tf_op jit(solution)/shard_map/pallas_call | solution.py:601
  19.7 3.7 %collective-permute-start.2 = (f32[888,128]{1,0:T(8,128)}, f32[888,128]{1,0:T(8,128)S(1)}, u32[]{:S(2)}, u32[]{:S(2)}) collective-permute-start(f32[888,128]{1,0:T(8,128)} %get-tuple-element.23), channel_id=1, source_target_pairs={{1,2},{17,18},{33,34},{49,50},{65,66},{81,82},{97,98},{113,114},{1... | collective-permute-start | bytes 1363976 | tf_op jit(solution)/shard_map/ppermute | solution.py:613
  23.4 0.1 collective-permute-start.3
  23.5 0.1 select_multiply_fusion
  23.6 1.9 %collective-permute-done.3.na_ref = f32[784,128]{1,0:T(8,128)S(1)} collective-permute-done((f32[784,128]{1,0:T(8,128)}, f32[784,128]{1,0:T(8,128)S(1)}, u32[]{:S(2)}, u32[]{:S(2)}) %collective-permute-start.3) | collective-permute-done | bytes 401440 | tf_op jit(solution)/shard_map/ppermute | solution.py:614
  25.5 0.1 broadcast_in_dim.23.fv_ref
  25.5 0.1 broadcast_in_dim.22.ft_ref
  25.6 9.0 %shard_map.88 = (f32[12,2,152,128]{3,2,1,0:T(8,128)S(1)}, f32[12,2,152,128]{3,2,1,0:T(8,128)S(1)}, f32[12,2,152,128]{3,2,1,0:T(8,128)S(1)}, f32[12,2,152,128]{3,...) custom-call(f32[39,96,128]{2,1,0:T(8,128)S(1)} %shard_map.85.low_own, ...), custom_call_target="tpu_custom_call" | custom-call | flops 40000000 | bytes 12000000 | tf_op jit(solution)/shard_map/pallas_call | solution.py:620
  34.6 4.9 %collective-permute-done.2.nb_ref = f32[888,128]{1,0:T(8,128)S(1)} collective-permute-done((f32[888,128]{1,0:T(8,128)}, f32[888,128]{1,0:T(8,128)S(1)}, u32[]{:S(2)}, u32[]{:S(2)}) %collective-permute-start.2) | collective-permute-done | bytes 454688 | tf_op jit(solution)/shard_map/ppermute | solution.py:613
  39.5 7.6 %shard_map.89 = (f32[12,96,128]{2,1,0:T(8,128)}, f32[12,96,128]{2,1,0:T(8,128)}, f32[96,128]{1,0:T(8,128)}) custom-call(f32[888,128]{1,0:T(8,128)S(1)} %collective-permute-done.2.nb_ref, f32[152,128]{1,0:T(8,128)S(1)} %broadcast_in_dim.22.ft_ref, f32[152,128]{1,0:T(8,128)S(1)} %broadcast_in_dim.23.fv_ref, f32[12,2,152,128]{3,2,1,0:T(8,128)S(1)} %get-tuple-element.25.u_in, ...), custom_call_target="tpu_custom_call" | custom-call | tf_op jit(solution)/shard_map/pallas_call | solution.py:628
  (4 shorter events, 0.0 us)
Async XLA Ops:
  0.6 12.5 %copy-start.5 = (s32[96,128]{1,0:T(8,128)S(1)}, s32[96,128]{1,0:T(8,128)}, u32[]{:S(2)}) copy-start(s32[96,128]{1,0:T(8,128)} %b_far.1) | copy-start | bytes 147460
  0.6 12.5 %copy-start.3 = (s32[12,96,128]{2,1,0:T(8,128)S(1)}, s32[12,96,128]{2,1,0:T(8,128)}, u32[]{:S(2)}) copy-start(s32[12,96,128]{2,1,0:T(8,128)} %m_far.1) | copy-start | bytes 1769476
  0.7 12.5 %copy-start.4 = (f32[96,128]{1,0:T(8,128)S(1)}, f32[96,128]{1,0:T(8,128)}, u32[]{:S(2)}) copy-start(f32[96,128]{1,0:T(8,128)} %s_far.1) | copy-start | bytes 147460
  0.7 12.5 %copy-start.2 = (f32[12,96,128]{2,1,0:T(8,128)S(1)}, f32[12,96,128]{2,1,0:T(8,128)}, u32[]{:S(2)}) copy-start(f32[12,96,128]{2,1,0:T(8,128)} %d_far.1) | copy-start | bytes 1769476
  0.7 12.5 %copy-start.1 = (f32[12,96,128]{2,1,0:T(8,128)S(1)}, f32[12,96,128]{2,1,0:T(8,128)}, u32[]{:S(2)}) copy-start(f32[12,96,128]{2,1,0:T(8,128)} %v_far.1) | copy-start | bytes 1769476
  0.7 12.5 %copy-start = (f32[12,96,128]{2,1,0:T(8,128)S(1)}, f32[12,96,128]{2,1,0:T(8,128)}, u32[]{:S(2)}) copy-start(f32[12,96,128]{2,1,0:T(8,128)} %u_far.1) | copy-start | bytes 1769476
  4.1 9.5 %collective-permute-start = (f32[5,96,128]{2,1,0:T(8,128)}, f32[5,96,128]{2,1,0:T(8,128)S(1)}, u32[]{:S(2)}, u32[]{:S(2)}) collective-permute-start(f32[5,96,128]{2,1,0:T(8,128)} %get-tuple-element.21), channel_id=1, source_target_pairs={{0,16},{16,0},{32,48},{48,32},{64,80},{80,64},{96,112},{112,96},{1... | collective-permute-start | bytes 737288 | tf_op jit(solution)/shard_map/ppermute | solution.py:590
  5.8 12.9 %collective-permute-start.1 = (f32[5,96,128]{2,1,0:T(8,128)}, f32[5,96,128]{2,1,0:T(8,128)S(1)}, u32[]{:S(2)}, u32[]{:S(2)}) collective-permute-start(f32[5,96,128]{2,1,0:T(8,128)} %get-tuple-element.22), channel_id=1, source_target_pairs={{0,240},{16,32},{32,16},{48,64},{64,48},{80,96},{96,80},{112,128},... | collective-permute-start | bytes 737288 | tf_op jit(solution)/shard_map/ppermute | solution.py:591
  19.7 19.8 %collective-permute-start.2 = (f32[888,128]{1,0:T(8,128)}, f32[888,128]{1,0:T(8,128)S(1)}, u32[]{:S(2)}, u32[]{:S(2)}) collective-permute-start(f32[888,128]{1,0:T(8,128)} %get-tuple-element.23), channel_id=1, source_target_pairs={{1,2},{17,18},{33,34},{49,50},{65,66},{81,82},{97,98},{113,114},{1... | collective-permute-start | bytes 1363976 | tf_op jit(solution)/shard_map/ppermute | solution.py:613
  23.4 2.0 %collective-permute-start.3 = (f32[784,128]{1,0:T(8,128)}, f32[784,128]{1,0:T(8,128)S(1)}, u32[]{:S(2)}, u32[]{:S(2)}) collective-permute-start(f32[784,128]{1,0:T(8,128)} %get-tuple-element.24), channel_id=1, source_target_pairs={{0,1},{16,17},{32,33},{48,49},{64,65},{80,81},{96,97},{112,113},{1... | collective-permute-start | bytes 1204232 | tf_op jit(solution)/shard_map/ppermute | solution.py:614

commit v5 on v4

--- a/solution.py
+++ b/solution.py
@@ -94,15 +94,16 @@
         own_ref[p] = plane
 
 
-def outer_rows(low_own, low_a, low_b, top_own, top_a, top_b, a_ref, c_ref):
+def outer_rows(own_ref, ea_ref, eb_ref, a_ref, c_ref):
     even = lax.rem(lax.axis_index("lat"), 2) == 0
     for p in range(SENT):
         if p < PLANES:
-            low, top = low_own[p], top_own[p]
+            ref, at = own_ref, p
         elif p < PLANES + PACKS:
-            low, top = low_a[p - PLANES], top_a[p - PLANES]
+            ref, at = ea_ref, p - PLANES
         else:
-            low, top = low_b[p - PLANES - PACKS], top_b[p - PLANES - PACKS]
+            ref, at = eb_ref, p - PLANES - PACKS
+        low, top = ref[at, pl.ds(0, 24), :], ref[at, pl.ds(ROWS - 24, 24), :]
         a_ref[pl.ds(p * HALO, HALO), :] = jnp.where(even, top[24 - HALO :], low[:HALO])
         c_ref[pl.ds(p * FOLD, FOLD), :] = jnp.where(even, low[:FOLD], top[24 - FOLD :])
 
@@ -526,7 +527,7 @@
     ghosts()
     end = jnp.where(even_lat, CORE[0], jnp.where(top, tiles, tiles - 2))
     lax.fori_loop(jnp.where(even_lat, 1, CORE[1]), end, tend, 0)
-    substeps(CHUNKS, top, flat, flow_u, flow_v, height)
+    substeps(((8, 40), (48, 40), (88, 48)), top, flat, flow_u, flow_v, height)
     low, high = OWN // 8, (OWN + ROWS) // 8
     here = jnp.where(even_lat, low, CORE[1]), jnp.where(even_lat, CORE[0], high)
     done = jnp.where(even_lat, CORE[0], low), jnp.where(even_lat, high, CORE[1])
@@ -566,10 +567,6 @@
     face = sign * jnp.sin(math.pi * ((row + 1.0) / cells - 0.5))
     wide = (TALL, LANES)
     return jnp.broadcast_to(centre[:, None], wide), jnp.broadcast_to(face[:, None], wide)
-
-
-def whole(*shape):
-    return pl.BlockSpec(shape, lambda *_: (0,) * len(shape))
 
 
 def shards(u_velocity, v_velocity, density, surface, land_mask, bottom):
@@ -596,19 +593,14 @@
         cost_estimate=pl.CostEstimate(flops=4000000, bytes_accessed=5000000, transcendentals=0),
     )(*fields)
 
-    low = lambda planes: pl.BlockSpec((planes, 24, LANES), lambda i: (0, 0, 0))
-    high = lambda planes: pl.BlockSpec((planes, 24, LANES), lambda i: (0, ROWS // 24 - 1, 0))
     rows_a, rows_b = pl.pallas_call(
         outer_rows,
-        grid=(1,),
-        in_specs=[low(PLANES), low(PACKS), low(PACKS), high(PLANES), high(PACKS), high(PACKS)],
-        out_specs=(whole(SENT * HALO, LANES), whole(888, LANES)),
         out_shape=(
             jax.ShapeDtypeStruct((SENT * HALO, LANES), f32),
             jax.ShapeDtypeStruct((888, LANES), f32),
         ),
-        compiler_params=params,
-    )(own, east_a, east_b, own, east_a, east_b)
+        compiler_params=pltpu.CompilerParams(vmem_limit_bytes=8 * 1024 * 1024),
+    )(own, east_a, east_b)
     lat_first, lat_second = lat_swaps()
     north_b = lax.ppermute(rows_b, ("lon", "lat"), lat_second)
     north_a = lax.ppermute(rows_a, ("lon", "lat"), lat_first)

time: 47.2 us -> 47.1 us (level)
  no operation moved by 1% of the time
where the time goes in v5:
time: 47.1 us; the launch traced here: 47 us
  Pallas kernels  21.2 us (45%)
  starting transfers between devices  12.8 us (27%)
  waiting for transfers between devices  11.9 us (25%)
  between operations  0.77 us (2%)
    pallas_call x1, Pallas kernels, shards(): pl.pallas_call(inner_rows, out_shape=tuple((jax.ShapeDtypeStruct(shape, f...  8.95 us
    pallas_call x1, Pallas kernels, shards(): pl.pallas_call(ocean_steps, out_shape=(jax.ShapeDtypeStruct(level_block,...  7.49 us
    ppermute x1, starting transfers between devices, shards(): east_b = lax.ppermute(pack_b, 'lon', lon_second)  7.3 us
    ppermute x1, waiting for transfers between devices, shards(): east_b = lax.ppermute(pack_b, 'lon', lon_second)  5.13 us
    ppermute x1, waiting for transfers between devices, shards(): north_b = lax.ppermute(rows_b, ('lon', 'lat'), lat_second)  4.9 us
    ppermute x1, starting transfers between devices, shards(): north_b = lax.ppermute(rows_b, ('lon', 'lat'), lat_second)  3.73 us
    pallas_call x1, Pallas kernels, shards(): pl.pallas_call(strips, out_shape=(jax.ShapeDtypeStruct((PACKS, ROWS, LANE...  3.42 us
    ppermute x1, waiting for transfers between devices, shards(): north_a = lax.ppermute(rows_a, ('lon', 'lat'), lat_first)  1.86 us
  transfers between devices with their start and end apart: 4, of which 3 were waited for; matrix products, arithmetic and copies ran while one was open for 0% of the time, Pallas kernels for 20%

profile of v5, /device:TPU:7, one launch (start us, length us, event | category | flops | bytes accessed | tf_op | source)
XLA Modules:
  0.0 47.0 jit_solution(15345066256229899251)
XLA Ops:
  0.6 0.0 copy-start.5
  0.6 0.0 copy-start.3
  0.7 0.0 copy-start.4
  0.7 0.0 copy-start.2
  0.7 0.0 copy-start.1
  0.7 0.0 copy-start
  0.7 3.4 %shard_map.86 = (f32[5,96,128]{2,1,0:T(8,128)}, f32[5,96,128]{2,1,0:T(8,128)}) custom-call(f32[12,96,128]{2,1,0:T(8,128)} %u_far.1, f32[12,96,128]{2,1,0:T(8,128)} %v_far.1, f32[12,96,128]{2,1,0:T(8,128)} %d_far.1, f32[96,128]{1,0:T(8,128)} %s_far.1, s32[12,96,128]{2,1,0:T(8,128)} %m_far.1, s32[96,128]{1,0:T(8,128)} %b_far.1), custom_call_target="tpu_custom_call" | custom-call | tf_op jit(solution)/shard_map/pallas_call | solution.py:577
  4.1 1.7 %collective-permute-start = (f32[5,96,128]{2,1,0:T(8,128)}, f32[5,96,128]{2,1,0:T(8,128)S(1)}, u32[]{:S(2)}, u32[]{:S(2)}) collective-permute-start(f32[5,96,128]{2,1,0:T(8,128)} %get-tuple-element.21), channel_id=1, source_target_pairs={{0,16},{16,0},{32,48},{48,32},{64,80},{80,64},{96,112},{112,96},{1... | collective-permute-start | bytes 737288 | tf_op jit(solution)/shard_map/ppermute | solution.py:587
  5.8 7.3 %collective-permute-start.1 = (f32[5,96,128]{2,1,0:T(8,128)}, f32[5,96,128]{2,1,0:T(8,128)S(1)}, u32[]{:S(2)}, u32[]{:S(2)}) collective-permute-start(f32[5,96,128]{2,1,0:T(8,128)} %get-tuple-element.22), channel_id=1, source_target_pairs={{0,240},{16,32},{32,16},{48,64},{64,48},{80,96},{96,80},{112,128},... | collective-permute-start | bytes 737288 | tf_op jit(solution)/shard_map/ppermute | solution.py:588
  13.1 0.0 copy-done.3
  13.2 0.0 copy-done.2
  13.2 0.4 shard_map.85.own_ref
  13.6 0.0 collective-permute-done.ea_ref
  13.6 5.1 %collective-permute-done.1.eb_ref = f32[5,96,128]{2,1,0:T(8,128)S(1)} collective-permute-done((f32[5,96,128]{2,1,0:T(8,128)}, f32[5,96,128]{2,1,0:T(8,128)S(1)}, u32[]{:S(2)}, u32[]{:S(2)}) %collective-permute-start.1) | collective-permute-done | bytes 245792 | tf_op jit(solution)/shard_map/ppermute | solution.py:588
  18.7 1.0 %shard_map.87 = (f32[784,128]{1,0:T(8,128)}, f32[888,128]{1,0:T(8,128)}) custom-call(f32[39,96,128]{2,1,0:T(8,128)S(1)} %shard_map.85.own_ref, f32[5,96,128]{2,1,0:T(8,128)S(1)} %collective-permute-done.ea_ref, f32[5,96,128]{2,1,0:T(8,128)S(1)} %collective-permute-done.1.eb_ref), custom_call_target="tpu_custom_call" | custom-call | tf_op jit(solution)/shard_map/pallas_call | solution.py:596
  19.7 3.7 %collective-permute-start.2 = (f32[888,128]{1,0:T(8,128)}, f32[888,128]{1,0:T(8,128)S(1)}, u32[]{:S(2)}, u32[]{:S(2)}) collective-permute-start(f32[888,128]{1,0:T(8,128)} %get-tuple-element.23), channel_id=1, source_target_pairs={{1,2},{17,18},{33,34},{49,50},{65,66},{81,82},{97,98},{113,114},{1... | collective-permute-start | bytes 1363976 | tf_op jit(solution)/shard_map/ppermute | solution.py:605
  23.4 0.1 collective-permute-start.3
  23.5 0.1 select_multiply_fusion
  23.6 1.9 %collective-permute-done.3.na_ref = f32[784,128]{1,0:T(8,128)S(1)} collective-permute-done((f32[784,128]{1,0:T(8,128)}, f32[784,128]{1,0:T(8,128)S(1)}, u32[]{:S(2)}, u32[]{:S(2)}) %collective-permute-start.3) | collective-permute-done | bytes 401440 | tf_op jit(solution)/shard_map/ppermute | solution.py:606
  25.5 0.1 broadcast_in_dim.23.fv_ref
  25.5 0.1 broadcast_in_dim.22.ft_ref
  25.6 9.0 %shard_map.88 = (f32[12,2,152,128]{3,2,1,0:T(8,128)S(1)}, f32[12,2,152,128]{3,2,1,0:T(8,128)S(1)}, f32[12,2,152,128]{3,2,1,0:T(8,128)S(1)}, f32[12,2,152,128]{3,...) custom-call(f32[39,96,128]{2,1,0:T(8,128)S(1)} %shard_map.85.own_ref, ...), custom_call_target="tpu_custom_call" | custom-call | flops 40000000 | bytes 12000000 | tf_op jit(solution)/shard_map/pallas_call | solution.py:612
  34.6 4.9 %collective-permute-done.2.nb_ref = f32[888,128]{1,0:T(8,128)S(1)} collective-permute-done((f32[888,128]{1,0:T(8,128)}, f32[888,128]{1,0:T(8,128)S(1)}, u32[]{:S(2)}, u32[]{:S(2)}) %collective-permute-start.2) | collective-permute-done | bytes 454688 | tf_op jit(solution)/shard_map/ppermute | solution.py:605
  39.5 7.5 %shard_map.89 = (f32[12,96,128]{2,1,0:T(8,128)}, f32[12,96,128]{2,1,0:T(8,128)}, f32[96,128]{1,0:T(8,128)}) custom-call(f32[888,128]{1,0:T(8,128)S(1)} %collective-permute-done.2.nb_ref, f32[152,128]{1,0:T(8,128)S(1)} %broadcast_in_dim.22.ft_ref, f32[152,128]{1,0:T(8,128)S(1)} %broadcast_in_dim.23.fv_ref, f32[12,2,152,128]{3,2,1,0:T(8,128)S(1)} %get-tuple-element.25.u_in, ...), custom_call_target="tpu_custom_call" | custom-call | tf_op jit(solution)/shard_map/pallas_call | solution.py:620
  (4 shorter events, 0.0 us)
Async XLA Ops:
  0.6 12.5 %copy-start.5 = (s32[96,128]{1,0:T(8,128)S(1)}, s32[96,128]{1,0:T(8,128)}, u32[]{:S(2)}) copy-start(s32[96,128]{1,0:T(8,128)} %b_far.1) | copy-start | bytes 147460
  0.6 12.5 %copy-start.3 = (s32[12,96,128]{2,1,0:T(8,128)S(1)}, s32[12,96,128]{2,1,0:T(8,128)}, u32[]{:S(2)}) copy-start(s32[12,96,128]{2,1,0:T(8,128)} %m_far.1) | copy-start | bytes 1769476
  0.7 12.5 %copy-start.4 = (f32[96,128]{1,0:T(8,128)S(1)}, f32[96,128]{1,0:T(8,128)}, u32[]{:S(2)}) copy-start(f32[96,128]{1,0:T(8,128)} %s_far.1) | copy-start | bytes 147460
  0.7 12.5 %copy-start.2 = (f32[12,96,128]{2,1,0:T(8,128)S(1)}, f32[12,96,128]{2,1,0:T(8,128)}, u32[]{:S(2)}) copy-start(f32[12,96,128]{2,1,0:T(8,128)} %d_far.1) | copy-start | bytes 1769476
  0.7 12.5 %copy-start.1 = (f32[12,96,128]{2,1,0:T(8,128)S(1)}, f32[12,96,128]{2,1,0:T(8,128)}, u32[]{:S(2)}) copy-start(f32[12,96,128]{2,1,0:T(8,128)} %v_far.1) | copy-start | bytes 1769476
  0.7 12.5 %copy-start = (f32[12,96,128]{2,1,0:T(8,128)S(1)}, f32[12,96,128]{2,1,0:T(8,128)}, u32[]{:S(2)}) copy-start(f32[12,96,128]{2,1,0:T(8,128)} %u_far.1) | copy-start | bytes 1769476
  4.1 9.5 %collective-permute-start = (f32[5,96,128]{2,1,0:T(8,128)}, f32[5,96,128]{2,1,0:T(8,128)S(1)}, u32[]{:S(2)}, u32[]{:S(2)}) collective-permute-start(f32[5,96,128]{2,1,0:T(8,128)} %get-tuple-element.21), channel_id=1, source_target_pairs={{0,16},{16,0},{32,48},{48,32},{64,80},{80,64},{96,112},{112,96},{1... | collective-permute-start | bytes 737288 | tf_op jit(solution)/shard_map/ppermute | solution.py:587
  5.8 12.9 %collective-permute-start.1 = (f32[5,96,128]{2,1,0:T(8,128)}, f32[5,96,128]{2,1,0:T(8,128)S(1)}, u32[]{:S(2)}, u32[]{:S(2)}) collective-permute-start(f32[5,96,128]{2,1,0:T(8,128)} %get-tuple-element.22), channel_id=1, source_target_pairs={{0,240},{16,32},{32,16},{48,64},{64,48},{80,96},{96,80},{112,128},... | collective-permute-start | bytes 737288 | tf_op jit(solution)/shard_map/ppermute | solution.py:588
  19.7 19.8 %collective-permute-start.2 = (f32[888,128]{1,0:T(8,128)}, f32[888,128]{1,0:T(8,128)S(1)}, u32[]{:S(2)}, u32[]{:S(2)}) collective-permute-start(f32[888,128]{1,0:T(8,128)} %get-tuple-element.23), channel_id=1, source_target_pairs={{1,2},{17,18},{33,34},{49,50},{65,66},{81,82},{97,98},{113,114},{1... | collective-permute-start | bytes 1363976 | tf_op jit(solution)/shard_map/ppermute | solution.py:605
  23.4 2.0 %collective-permute-start.3 = (f32[784,128]{1,0:T(8,128)}, f32[784,128]{1,0:T(8,128)S(1)}, u32[]{:S(2)}, u32[]{:S(2)}) collective-permute-start(f32[784,128]{1,0:T(8,128)} %get-tuple-element.24), channel_id=1, source_target_pairs={{0,1},{16,17},{32,33},{48,49},{64,65},{80,81},{96,97},{112,113},{1... | collective-permute-start | bytes 1204232 | tf_op jit(solution)/shard_map/ppermute | solution.py:606
